TPU v7x, 128 devices: a whole 4x4x4 slice. The times are simulated.
128 devices in a mesh: dom: 64 (over z, x, y_lo, core), hid: 2 (over y_hi).
Axes of the slice: x: 4, y: 4 (y_hi: 2, y_lo: 2; y = y_hi * 2 + y_lo), z: 4, core: 2. Of those that a mesh axis runs over, the one named last changes fastest.
Arguments:
- node_latent: bfloat16 [16384, 512], P('dom'), may hold values from -6 to 6
- edge_latent: bfloat16 [65536, 512], P('dom'), may hold values from -6 to 6
- send_rows: int32 [64, 2, 64], P('dom'), may hold values from 0 to 255, as said below
- edge_src: int32 [65536], P('dom'), may hold values from 0 to 383, as said below
- edge_dst: int32 [65536], P('dom'), may hold values from 0 to 255
- edge_live: int32 [64], P('dom'), may hold values from 512 to 1024, as said below
- w_in_blocks: bfloat16 [1536, 1536], P(None, 'hid'), may hold values from -0.15625 to 0.15625
- w_in_scale: float32 [12, 12], P(None, 'hid'), may hold values from 0.25 to 4
- bias_in: float32 [1536], P('hid'), may hold values from -4 to 4
- w_out_blocks: bfloat16 [1536, 512], P('hid'), may hold values from -0.15625 to 0.15625
- w_out_scale: float32 [12, 4], P('hid'), may hold values from 0.25 to 4
- bias_out: float32 [512], replicated, may hold values from -4 to 4
- norm_gain: float32 [512], replicated, may hold values from 0.1 to 1.9
- grad_edge: bfloat16 [65536, 512], P('dom'), may hold values from -6 to 6
- grad_agg: bfloat16 [16384, 512], P('dom'), may hold values from -6 to 6
Outputs:
- grad_edge_in: bfloat16 [65536, 512], P(('dom', 'hid'))
- grad_node: bfloat16 [16384, 512], P('dom', 'hid')
- grad_w_in: float32 [1536, 1536], P(None, 'hid')
- grad_bias_in: float32 [1536], P('hid')
- grad_w_out: float32 [1536, 512], P('hid')
- grad_vectors: float32 [3, 512], replicated
Inputs may be any that keep to these rules, and one draw needn't show every extreme that they name: send_rows[p, 0] and send_rows[p, 1] together name 128 distinct nodes of partition p. `edge_src`: rows below 256 are the partition's own nodes, the next 64 rows come from the partition below, the last 64 from the partition above; the first partition names no row of the middle range, the last partition none of the upper range. `edge_live`: live edges come first in each partition's block; at least one partition is full and at least one is half full.
All inputs are finite; a program needn't handle non-finite values.
Results may differ from a plain program's by a relative error of at most 0.007.
Values may be sent and summed in bfloat16 or wider, within the bound.
A program may use at most 128 MiB of HBM per device.

v0:
```python
import jax
import jax.numpy as jnp
from jax import lax
from jax.sharding import PartitionSpec as P

EPS = 1e-05


def passed_along(block, axis, distance):
    devices = range(lax.axis_size(axis))
    route = [(i - distance, i) for i in devices if i - distance in devices]
    return lax.ppermute(block, axis, route)


def dequantize(blocks, scales):
    row_repeat = blocks.shape[0] // scales.shape[0]
    col_repeat = blocks.shape[1] // scales.shape[1]
    spread = jnp.repeat(jnp.repeat(scales, row_repeat, axis=0), col_repeat, axis=1)
    return (blocks.astype(jnp.float32) * spread).astype(jnp.bfloat16)


def norm_backward(message, gain, upstream):
    centre = message - jnp.mean(message, axis=1, keepdims=True)
    inverse = lax.rsqrt(jnp.mean(centre * centre, axis=1, keepdims=True) + EPS)
    normed = centre * inverse
    scaled = upstream * gain
    grad_message = inverse * (
        scaled
        - jnp.mean(scaled, axis=1, keepdims=True)
        - normed * jnp.mean(scaled * normed, axis=1, keepdims=True)
    )
    return (normed, grad_message)


def silu_slope(pre_act):
    sigma = jax.nn.sigmoid(pre_act)
    return sigma * (1.0 + pre_act * (1.0 - sigma))


def contract_rows(left_side, right_side):
    return lax.dot_general(
        left_side, right_side, (((0,), (0,)), ((), ())), preferred_element_type=jnp.float32
    )


def contract_cols(left_side, right_side):
    return lax.dot_general(
        left_side, right_side, (((1,), (1,)), ((), ())), preferred_element_type=jnp.float32
    )


def collect_rows(values, node_ids, table_rows):
    one_hot = (lax.iota(jnp.int32, table_rows)[:, None] == node_ids[None, :]).astype(jnp.float32)
    return jnp.dot(
        one_hot, values, preferred_element_type=jnp.float32, precision=lax.Precision.HIGHEST
    )


def per_device(
    node_latent,
    edge_latent,
    send_rows,
    edge_src,
    edge_dst,
    edge_live,
    w_in_blocks,
    w_in_scale,
    bias_in,
    w_out_blocks,
    w_out_scale,
    bias_out,
    norm_gain,
    grad_edge,
    grad_agg,
):
    latent_width = node_latent.shape[1]
    own_nodes = node_latent.shape[0]
    edge_rows = edge_latent.shape[0]
    shared = send_rows.shape[2]
    send_lists = send_rows[0]
    factor = 1.0 / edge_rows
    rows_down = jnp.take(node_latent, send_lists[0], axis=0)
    rows_up = jnp.take(node_latent, send_lists[1], axis=0)
    from_lower = passed_along(rows_up, "dom", 1)
    from_upper = passed_along(rows_down, "dom", -1)
    extended = jnp.concatenate([node_latent, from_lower, from_upper], axis=0)
    inputs = jnp.concatenate(
        [
            edge_latent,
            jnp.take(extended, edge_src, axis=0),
            jnp.take(node_latent, edge_dst, axis=0),
        ],
        axis=1,
    )
    w_first = dequantize(w_in_blocks, w_in_scale)
    w_second = dequantize(w_out_blocks, w_out_scale)
    pre_act = jnp.dot(inputs, w_first, preferred_element_type=jnp.float32) + bias_in
    activated = jax.nn.silu(pre_act).astype(jnp.bfloat16)
    partial_out = jnp.dot(activated, w_second, preferred_element_type=jnp.float32)
    message = lax.psum(partial_out, "hid") + bias_out
    live_mask = (lax.iota(jnp.int32, edge_rows) < edge_live[0]).astype(jnp.float32)[:, None]
    upstream = (
        grad_edge.astype(jnp.float32) + jnp.take(grad_agg, edge_dst, axis=0).astype(jnp.float32)
    ) * live_mask
    normed, grad_message = norm_backward(message, norm_gain, upstream)
    vectors = (
        jnp.stack(
            [
                jnp.sum(grad_message, axis=0),
                jnp.sum(upstream * normed, axis=0),
                jnp.sum(upstream, axis=0),
            ]
        )
        * factor
    )
    grad_message_low = grad_message.astype(jnp.bfloat16)
    grad_w_second = contract_rows(activated, grad_message_low) * factor
    grad_act = contract_cols(grad_message_low, w_second)
    grad_pre = grad_act * silu_slope(pre_act)
    grad_bias_local = jnp.sum(grad_pre, axis=0) * factor
    grad_pre_low = grad_pre.astype(jnp.bfloat16)
    grad_w_first = contract_rows(inputs, grad_pre_low) * factor
    half_rows = edge_rows // lax.axis_size("hid")
    first_edge = lax.axis_index("hid") * half_rows
    my_upstream = lax.dynamic_slice_in_dim(upstream, first_edge, half_rows, 0)
    summed = lax.psum_scatter(
        contract_cols(grad_pre_low, w_first), "hid", scatter_dimension=0, tiled=True
    )
    own_edge = summed[:, :latent_width]
    my_sources = lax.dynamic_slice_in_dim(edge_src, first_edge, half_rows, 0)
    my_targets = lax.dynamic_slice_in_dim(edge_dst, first_edge, half_rows, 0)
    node_data = jnp.concatenate(
        [summed[:, latent_width : 2 * latent_width], summed[:, 2 * latent_width :]], axis=0
    )
    node_ids = jnp.concatenate([my_sources, my_targets], axis=0)
    grad_edge_in = (my_upstream + own_edge).astype(jnp.bfloat16)
    node_partial = collect_rows(node_data, node_ids, own_nodes + 2 * shared)
    node_summed = lax.psum_scatter(node_partial, "hid", scatter_dimension=1, tiled=True)
    lower_ghost = node_summed[own_nodes : own_nodes + shared]
    upper_ghost = node_summed[own_nodes + shared :]
    back_from_upper = passed_along(lower_ghost.astype(jnp.bfloat16), "dom", -1).astype(
        lower_ghost.dtype
    )
    back_from_lower = passed_along(upper_ghost.astype(jnp.bfloat16), "dom", 1).astype(
        upper_ghost.dtype
    )
    grad_node = (
        node_summed[:own_nodes]
        .at[send_lists[1]]
        .add(back_from_upper)
        .at[send_lists[0]]
        .add(back_from_lower)
    )
    grad_w_first, grad_bias_local, grad_w_second, vectors = lax.psum(
        (grad_w_first, grad_bias_local, grad_w_second, vectors), "dom"
    )
    return (
        grad_edge_in,
        grad_node.astype(jnp.bfloat16),
        grad_w_first,
        grad_bias_local,
        grad_w_second,
        vectors,
    )


def solution(mesh):
    in_specs = (
        P("dom", None),
        P("dom", None),
        P("dom", None, None),
        P("dom"),
        P("dom"),
        P("dom"),
        P(None, "hid"),
        P(None, "hid"),
        P("hid"),
        P("hid", None),
        P("hid", None),
        P(),
        P(),
        P("dom", None),
        P("dom", None),
    )
    out_specs = (
        P(("dom", "hid"), None),
        P("dom", "hid"),
        P(None, "hid"),
        P("hid"),
        P("hid", None),
        P(),
    )
    return jax.shard_map(
        per_device, mesh=mesh, in_specs=in_specs, out_specs=out_specs, check_vma=False
    )
```

profile of v0, /device:TPU:1, one launch (start us, length us, event | category | flops | bytes accessed | tf_op | source)
XLA Modules:
  0.0 825.8 jit_solution(1861118909738004381)
XLA Ops:
  8.0 1.7 gather_fusion.3
  9.8 3.3 collective-permute-start.1
  13.2 1.7 gather_fusion.2
  14.9 3.2 collective-permute-start
  20.3 4.0 gather_fusion.4
  24.3 1.2 broadcast_select_fusion
  25.5 2.8 copy.23
  28.5 1.9 fusion
  30.4 4.0 gather_fusion
  35.9 6.3 multiply_convert_fusion
  44.3 2.3 fusion.27
  47.4 4.0 gather_fusion.1
  51.4 70.6 %all-reduce.5.cloned.1.call-done = f32[1024,512]{1,0:T(8,128)} async-done(((f32[1024,512]{1,0:T(8,128)}), f32[1024,512]{1,0:T(8,128)}) %all-reduce.5.cloned.1.call-update) | async-done | bytes 2097168 | tf_op jit(solution)/shard_map/psum | solution.py:100
  122.0 2.0 add_reduce_fusion
  124.8 1.9 multiply_reduce_fusion
  128.3 1.6 fusion.32
  130.0 1.1 copy-done.26
  131.1 4.6 fusion.10
  136.6 79.9 %reduce-scatter.3.cloned.1.call-done = f32[512,1536]{1,0:T(8,128)} async-done(((f32[1024,1536]{1,0:T(8,128)}), f32[512,1536]{1,0:T(8,128)}) %reduce-scatter.3.cloned.1.call-update) | async-done | bytes 3145744 | tf_op jit(solution)/shard_map/reduce_scatter | solution.py:126
  216.4 3.0 fusion.30
  219.4 2.6 fusion.1
  222.2 3.5 convolution_multiply_fusion.1
  225.8 4.9 convolution_multiply_fusion
  231.4 11.8 %reduce-scatter.5.cloned.1.call-done = f32[384,256]{1,0:T(8,128)} async-done(((f32[384,512]{1,0:T(8,128)}), f32[384,256]{1,0:T(8,128)}) %reduce-scatter.5.cloned.1.call-update) | async-done | bytes 393232 | tf_op jit(solution)/shard_map/reduce_scatter | solution.py:138
  244.2 2.6 collective-permute-start.2
  246.8 3.0 collective-permute-start.3
  249.8 272.6 %all-reduce = (f32[768]{0:T(1024)}, f32[3,512]{1,0:T(4,128)}) all-reduce(f32[768]{0:T(1024)S(1)} %broadcast_multiply_fusion, f32[3,512]{1,0:T(4,128)S(1)} %maximum_multiply_fusion), channel_id=1, replica_groups=mesh['dom'=64,'hid'=2] {'dom'}, use_global_device_ids=true, to_apply=%region_11.14 | all-reduce | flops 2304 | bytes 18432 | tf_op jit(solution)/shard_map/psum | solution.py:154
  523.3 1.1 scatter_custom_fusion
  524.4 1.1 scatter_custom_fusion.1
  526.2 287.0 %all-reduce.7.cloned.1.call-done = (f32[1536,768]{1,0:T(8,128)}, f32[768,512]{1,0:T(8,128)}) async-done(((f32[1536,768]{1,0:T(8,128)}, f32[768,512]{1,0:T(8,128)}), (f32[1536,768]{1,0:T(8,128)}, f32[768,512]{1,0:T(8,128)})) %all-reduce.7.cloned.1.call-update) | async-done | bytes 6291472 | tf_op jit(solution)/shard_map/psum | solution.py:154
  813.2 4.9 copy.40
  818.2 1.1 copy.41
  (101 shorter events, 13.7 us)
Async XLA Ops:
  7.2 40.2 %copy-start = (bf16[256,512]{1,0:T(8,128)(2,1)S(1)}, bf16[256,512]{1,0:T(8,128)(2,1)}, u32[]{:S(2)}) copy-start(bf16[256,512]{1,0:T(8,128)(2,1)} %param.33) | copy-start | bytes 786436
  7.2 13.1 %copy-start.1 = (bf16[256,512]{1,0:T(8,128)(2,1)S(1)}, bf16[256,512]{1,0:T(8,128)(2,1)}, u32[]{:S(2)}) copy-start(bf16[256,512]{1,0:T(8,128)(2,1)} %param.19) | copy-start | bytes 786436
  7.2 114.8 %all-reduce.5.cloned.1.call-start = ((), (), s32[]{:S(2)}) async-start(), calls=%async_computation.2 | async-start | bytes 4194304 | tf_op jit(solution)/shard_map/psum | solution.py:100
  9.8 20.5 %collective-permute-start.1 = (bf16[64,512]{1,0:T(8,128)(2,1)S(1)}, bf16[64,512]{1,0:T(8,128)(2,1)S(1)}, u32[]{:S(2)}, u32[]{:S(2)}) collective-permute-start(bf16[64,512]{1,0:T(8,128)(2,1)S(1)} %broadcast_select_fusion.2), channel_id=1, source_target_pairs={{2,0},{4,2},{6,4},{8,6},{10,8},{12,10},{14,12},{16,14},{18,16},{20... | collective-permute-start | bytes 196616 | tf_op jit(solution)/shard_map/ppermute | solution.py:12
  14.9 15.4 %collective-permute-start = (bf16[64,512]{1,0:T(8,128)(2,1)S(1)}, bf16[64,512]{1,0:T(8,128)(2,1)S(1)}, u32[]{:S(2)}, u32[]{:S(2)}) collective-permute-start(bf16[64,512]{1,0:T(8,128)(2,1)S(1)} %broadcast_select_fusion.3), channel_id=1, source_target_pairs={{0,2},{2,4},{4,6},{6,8},{8,10},{10,12},{12,14},{14,16},{16,18},{18... | collective-permute-start | bytes 196616 | tf_op jit(solution)/shard_map/ppermute | solution.py:12
  20.3 4.0 copy-start.19
  25.5 2.9 copy-start.22
  30.4 4.2 copy-start.25
  34.3 1.2 copy-start.9
  34.4 1.5 copy-start.23
  35.9 6.3 copy-start.11
  42.2 2.2 copy-start.15
  46.7 169.7 %reduce-scatter.3.cloned.1.call-start = ((), (), s32[]{:S(2)}) async-start(), calls=%async_computation.3 | async-start | bytes 9437184 | tf_op jit(solution)/shard_map/reduce_scatter | solution.py:126
  47.4 74.6 %copy-start.17 = (f32[512]{0:T(512)S(1)}, f32[512]{0:T(512)}, u32[]{:S(2)}) copy-start(f32[512]{0:T(512)} %param.30) | copy-start | bytes 6148
  51.4 73.3 %copy-start.20 = (f32[512]{0:T(512)S(1)}, f32[512]{0:T(512)}, u32[]{:S(2)}) copy-start(f32[512]{0:T(512)} %param.31) | copy-start | bytes 6148
  122.0 2.2 copy-start.2
  122.0 2.8 copy-start.13
  124.7 2.9 copy-start.28
  126.7 1.4 copy-start.4
  126.7 1.6 copy-start.16
  127.6 2.3 copy-start.14
  128.3 2.8 copy-start.7
  135.7 107.4 %reduce-scatter.5.cloned.1.call-start = ((), (), s32[]{:S(2)}) async-start(), calls=%async_computation.4 | async-start | bytes 1179648 | tf_op jit(solution)/shard_map/reduce_scatter | solution.py:138
  219.4 2.7 copy-start.6
  222.1 3.7 copy-start.10
  222.1 591.1 %all-reduce.7.cloned.1.call-start = ((), (), s32[]{:S(2)}) async-start(), calls=%async_computation.5 | async-start | bytes 12582912 | tf_op jit(solution)/shard_map/psum | solution.py:154
  222.2 3.6 copy-start.12
  222.2 3.6 copy-start.24
  222.2 3.6 copy-start.27
  244.2 279.2 %collective-permute-start.2 = (bf16[64,256]{1,0:T(8,128)(2,1)S(1)}, bf16[64,256]{1,0:T(8,128)(2,1)S(1)}, u32[]{:S(2)}, u32[]{:S(2)}) collective-permute-start(bf16[64,256]{1,0:T(8,128)(2,1)S(1)} %get-tuple-element.27), channel_id=1, source_target_pairs={{2,0},{4,2},{6,4},{8,6},{10,8},{12,10},{14,12},{16,14},{18,16},{20... | collective-permute-start | bytes 98312 | tf_op jit(solution)/shard_map/ppermute | solution.py:12
  246.8 277.7 %collective-permute-start.3 = (bf16[64,256]{1,0:T(8,128)(2,1)S(1)}, bf16[64,256]{1,0:T(8,128)(2,1)S(1)}, u32[]{:S(2)}, u32[]{:S(2)}) collective-permute-start(bf16[64,256]{1,0:T(8,128)(2,1)S(1)} %get-tuple-element.26), channel_id=1, source_target_pairs={{0,2},{2,4},{4,6},{6,8},{8,10},{10,12},{12,14},{14,16},{16,18},{18... | collective-permute-start | bytes 98312 | tf_op jit(solution)/shard_map/ppermute | solution.py:12
  813.2 4.9 copy-start.8
  (5 other events, 4.8 us)
Sparse Core Ops, SparseCore 0:
  46.8 75.1 all-reduce.4
  135.9 80.5 reduce-scatter.2
  222.2 20.8 reduce-scatter.4
  246.3 566.8 all-reduce.6
where the time goes:
time: 827 us; the launch traced here: 826 us
  waiting for transfers between devices  449 us (54%)
  blocking collectives  273 us (33%)
  local copies, waits for them, and re-layouts  32.9 us (4%)
  matrix products  25.9 us (3%)
  other arithmetic  17.8 us (2%)
  between operations  14.9 us (2%)
  starting transfers between devices  12.4 us (1%)
    psum x1, waiting for transfers between devices, per_device(): lax.psum((grad_w_first, grad_bias_local, grad_w_second, vectors), 'dom')  287 us
    psum x1, blocking collectives, per_device(): lax.psum((grad_w_first, grad_bias_local, grad_w_second, vectors), 'dom')  273 us
    reduce_scatter x1, waiting for transfers between devices, per_device(): lax.psum_scatter(contract_cols(grad_pre_low, w_first), 'hid', scatter_dim...  79.9 us
    psum x1, waiting for transfers between devices, per_device(): message = lax.psum(partial_out, 'hid') + bias_out  70.6 us
  transfers between devices with their start and end apart: 8, of which 4 were waited for; matrix products, arithmetic and copies ran while one was open for 4% of the time, Pallas kernels for 0%

commit v1 on v0

v1 whole, which is shorter than its diff:
```python
import jax
import jax.numpy as jnp
from jax import lax
from jax.experimental import pallas as pl
from jax.experimental.pallas import tpu as pltpu
from jax.sharding import PartitionSpec as P

EPS = 1e-05
MESH = pl.DeviceIdType.MESH
F32 = jnp.float32
BF16 = jnp.bfloat16
CHUNKS = 6
LIMIT = 60 << 20


class Place:
    def __init__(self):
        dom = lax.axis_index("dom")
        self.hid = lax.axis_index("hid")
        self.dom = dom
        self.z = lax.div(dom, 16)
        self.x = lax.rem(lax.div(dom, 4), 4)
        self.yl = lax.rem(lax.div(dom, 2), 2)
        self.y = 2 * self.hid + self.yl
        self.core = lax.rem(dom, 2)

    def at(self, z=None, x=None, y=None, core=None):
        z = self.z if z is None else z
        x = self.x if x is None else x
        y = self.y if y is None else y
        core = self.core if core is None else core
        return (((z * 4 + x) * 2 + lax.rem(y, 2)) * 2 + core, lax.div(y, 2))

    def ring(self, axis, step):
        return self.at(**{axis: lax.rem(getattr(self, axis) + step, 4)})

    def other_core(self):
        return self.at(core=1 - self.core)

    def cross(self):
        return self.at(y=3 - self.y)

    def pair(self):
        return self.at(y=self.y + 1 - 2 * self.yl)

    def partition(self, step):
        return (lax.rem(self.dom + step, 64), self.hid)


def ready(partners):
    barrier = pltpu.get_barrier_semaphore()
    for partner in partners:
        pl.semaphore_signal(barrier, inc=1, device_id=partner, device_id_type=MESH)
    pl.semaphore_wait(barrier, len(partners))


def remote(src, dst, send_sem, recv_sem, target):
    return pltpu.make_async_remote_copy(
        src_ref=src,
        dst_ref=dst,
        send_sem=send_sem,
        recv_sem=recv_sem,
        device_id=target,
        device_id_type=MESH,
    )


def kind(chunk):
    return chunk % 3


def own_tile(place, chunk, yl=None):
    yl = place.yl if yl is None else yl
    if kind(chunk) == 0:
        return (place.z * 4 + place.x) * 2 + yl
    if kind(chunk) == 1:
        return (place.x * 2 + yl) * 4 + place.z
    return (yl * 4 + place.z) * 4 + place.x


def rows_of(first, count, unit=16):
    return pl.ds(pl.multiple_of(first * unit, unit), count * unit)


def gather_steps(place, chunk):
    z, x, yl = place.z, place.x, place.yl
    z_ring = [place.ring("z", j) for j in (1, 2, 3)]
    x_ring = [place.ring("x", j) for j in (1, 2, 3)]
    pair = [place.pair()]
    if kind(chunk) == 0:
        return [
            ((z * 4 + x) * 2 + yl, 1, pair),
            ((z * 4 + x) * 2, 2, x_ring),
            (z * 8, 8, z_ring),
        ]
    if kind(chunk) == 1:
        return [
            ((x * 2 + yl) * 4 + z, 1, z_ring),
            ((x * 2 + yl) * 4, 4, pair),
            (x * 8, 8, x_ring),
        ]
    return [
        ((yl * 4 + z) * 4 + x, 1, x_ring),
        ((yl * 4 + z) * 4, 4, z_ring),
        (yl * 16, 16, pair),
    ]


class Gather:
    def __init__(self, place, buf, send_sem, recv_sem):
        self.place, self.buf = place, buf
        self.send_sem, self.recv_sem = send_sem, recv_sem
        self.steps = {}
        self.flying = {}

    def start(self, chunk, step):
        place = self.place
        if chunk not in self.steps:
            self.steps[chunk] = gather_steps(place, chunk)
        block = 2 * chunk + place.core
        if step == 3:
            first, count, targets = 0, 32, [place.other_core()]
            base = 7
        else:
            first, count, targets = self.steps[chunk][step]
            base = sum(len(s[2]) for s in self.steps[chunk][:step])
        part = self.buf.at[block, rows_of(first, count)]
        copies = []
        for j, target in enumerate(targets):
            copy = remote(
                part, part, self.send_sem.at[chunk, base + j], self.recv_sem.at[chunk, base + j], target
            )
            copy.start()
            copies.append(copy)
        self.flying[chunk, step] = copies

    def arrived(self, chunk, step):
        for copy in self.flying[chunk, step]:
            copy.wait_recv()

    def sent(self):
        for copies in self.flying.values():
            for copy in copies:
                copy.wait_send()


RING = (1, 2, 3)
REDUCE_AXES = {0: ("z", "x", "y"), 1: ("x", "y", "z"), 2: ("y", "z", "x")}


def dequantize(own, w_in_ref, w_in_scale, w_out_ref, w_out_scale):
    def block(index, _):
        j = lax.div(index, 3)
        r = lax.rem(index, 3)
        for a in range(4):
            for b in range(2):
                scale = w_in_scale[4 * r + a, 2 * j + b]
                rows = pl.ds(pl.multiple_of(512 * r + 128 * a, 128), 128)
                cols = pl.ds(pl.multiple_of(256 * j + 128 * b, 128), 128)
                value = w_in_ref[rows, cols].astype(F32) * scale
                own[3 + index, 128 * a : 128 * a + 128, 128 * b : 128 * b + 128] = value.astype(BF16)
        return 0

    for a in range(6):
        for b in range(4):
            scale = w_out_scale[a, b]
            value = w_out_ref[128 * a : 128 * a + 128, 128 * b : 128 * b + 128].astype(F32) * scale
            if a < 4:
                index, row = b // 2, 128 * a
            else:
                index, row = 2, 128 * (a - 4) + 256 * (b // 2)
            col = 128 * (b % 2)
            own[index, row : row + 128, col : col + 128] = value.astype(BF16)
    lax.fori_loop(0, 9, block, 0)


def weights_kernel(
    w_in_ref,
    w_in_scale,
    w_out_ref,
    w_out_scale,
    bias_ref,
    node_ref,
    send_ref,
    weights,
    bias,
    halo,
    halo_out,
    gather_send,
    gather_recv,
    cross_send,
    cross_recv,
    halo_send,
    halo_recv,
):
    place = Place()
    partners = [place.ring("z", j) for j in RING] + [place.ring("x", j) for j in RING]
    partners += [place.pair(), place.other_core(), place.cross()]
    partners += [place.partition(1), place.partition(63)]
    ready(partners)
    own, other = weights.at[0], weights.at[1]
    dequantize(own, w_in_ref, w_in_scale, w_out_ref, w_out_scale)
    bias[0] = jnp.zeros((8, 256), F32)
    bias[0, 0:3, :] = bias_ref[...]
    copies = []
    crossing = {}
    copy = remote(bias.at[0], bias.at[1], cross_send.at[6], cross_recv.at[6], place.cross())
    copy.start()
    bias_copy = copy
    for chunk in (2, 3, 4, 5, 0, 1):
        block = 2 * chunk + place.core
        if chunk < 2:
            rows = slice(None)
        else:
            rows = rows_of(own_tile(place, chunk, 1 - place.yl), 1)
        copy = remote(
            own.at[block, rows],
            other.at[block, rows],
            cross_send.at[chunk],
            cross_recv.at[chunk],
            place.cross(),
        )
        copy.start()
        crossing[chunk] = copy
    for side in (0, 1):
        picks = (lax.broadcasted_iota(jnp.int32, (256, 64), 0) == send_ref[side : side + 1, :]).astype(F32)
        halo_out[side] = lax.dot_general(
            picks.astype(BF16), node_ref[...], (((0,), (0,)), ((), ())), preferred_element_type=F32
        ).astype(BF16)
    up = remote(halo_out.at[1], halo.at[0], halo_send.at[0], halo_recv.at[0], place.partition(1))
    down = remote(halo_out.at[0], halo.at[1], halo_send.at[1], halo_recv.at[1], place.partition(63))
    up.start()
    down.start()
    gather = Gather(place, other, gather_send, gather_recv)
    for step in range(4):
        for chunk in (2, 3, 4, 5):
            if step == 0:
                crossing[chunk].wait_recv()
            else:
                gather.arrived(chunk, step - 1)
            gather.start(chunk, step)
    for chunk in (0, 1):
        crossing[chunk].wait_recv()
        gather.start(chunk, 3)
    for chunk in range(CHUNKS):
        gather.arrived(chunk, 3)
    bias_copy.wait_recv()
    up.wait_recv()
    down.wait_recv()
    gather.sent()
    for copy in list(crossing.values()) + [bias_copy, up, down]:
        copy.wait_send()


def place_rows(grads, block, first, value, half):
    count = value.shape[0]
    group = {0: 32, 1: 128, 2: 512}[kind(block // 2)]
    for at in range(0, count, min(group, count)):
        row = first + at
        base = (row // group) * 2 * group + row % group
        size = min(group, count)
        grads[block, pl.ds(pl.multiple_of(base + group * half, 32), size), :] = value[at : at + size]


def compute_kernel(
    edge_ref,
    gedge_ref,
    node_ref,
    gagg_ref,
    halo,
    src_ref,
    dst_ref,
    live_ref,
    weights,
    bias,
    bias_out_ref,
    gain_ref,
    grad_edge_ref,
    grads,
    own_table,
    halo_table,
    sums,
    inp,
    inpt,
    ext,
    pick_src,
    pick_dst,
    act,
    slope,
    up,
    msg,
    low,
    pre_low,
    gedge,
    sem,
):
    hid = lax.axis_index("hid")
    dom = lax.axis_index("dom")
    first_edge = pl.multiple_of(hid * 512, 512)
    get_edge = pltpu.make_async_copy(edge_ref.at[pl.ds(first_edge, 512)], inp.at[0], sem.at[0])
    get_cot = pltpu.make_async_copy(gedge_ref.at[pl.ds(first_edge, 512)], gedge, sem.at[1])
    get_edge.start()
    get_cot.start()
    ext[0:256] = node_ref[...]
    ext[256:320] = jnp.where(dom > 0, halo[0], jnp.zeros((64, 512), BF16))
    ext[320:384] = jnp.where(dom < 63, halo[1], jnp.zeros((64, 512), BF16))
    for k in range(4):
        cols = slice(128 * k, 128 * k + 128)
        src_row = src_ref[pl.ds(4 * hid + k, 1), :]
        dst_row = dst_ref[pl.ds(4 * hid + k, 1), :]
        pick_src[:, cols] = (lax.broadcasted_iota(jnp.int32, (384, 128), 0) == src_row).astype(F32).astype(BF16)
        pick_dst[:, cols] = (lax.broadcasted_iota(jnp.int32, (256, 128), 0) == dst_row).astype(F32).astype(BF16)

    def tdot(a, b):
        return lax.dot_general(a, b, (((0,), (0,)), ((), ())), preferred_element_type=F32)

    def ndot(a, b):
        return lax.dot_general(a, b, (((1,), (1,)), ((), ())), preferred_element_type=F32)

    def dot(a, b):
        return jnp.dot(a, b, preferred_element_type=F32)

    inp[1] = tdot(pick_src[...], ext[...]).astype(BF16)
    inp[2] = tdot(pick_dst[...], node_ref[...]).astype(BF16)
    up[...] = tdot(pick_dst[...], gagg_ref[...])
    get_edge.wait()
    get_cot.wait()
    for r in range(3):
        inpt[r] = inp[r].T

    for slot in range(2):

        def forward(j, _):
            pre = bias[slot, pl.ds(j, 1), :]
            for r in range(3):
                pre = pre + dot(inp[r], weights[slot, 3 + 3 * j + r])
            sigma = 1.0 / (1.0 + jnp.exp(-pre))
            value = pre * sigma
            act[3 * slot + j] = value.astype(BF16)
            slope[3 * slot + j] = sigma + value * (1.0 - sigma)
            return 0

        lax.fori_loop(0, 3, forward, 0)

    for side in range(2):
        total = bias_out_ref[:, 256 * side : 256 * side + 256]
        for slot in range(2):
            for j in range(2):
                total = total + dot(act[3 * slot + j], weights[slot, side, 256 * j : 256 * j + 256, :])
            total = total + dot(act[3 * slot + 2], weights[slot, 2, 256 * side : 256 * side + 256, :])
        msg[:, 256 * side : 256 * side + 256] = total

    live = live_ref[0] - hid * 512
    gain = gain_ref[...]

    def norm(i, carry):
        rows = pl.ds(pl.multiple_of(i * 64, 64), 64)
        mask = (lax.broadcasted_iota(jnp.int32, (64, 512), 0) + i * 64) < live
        upstream = jnp.where(mask, gedge[rows, :].astype(F32) + up[rows, :], 0.0)
        up[rows, :] = upstream
        message = msg[rows, :]
        centre = message - jnp.mean(message, axis=1, keepdims=True)
        inverse = lax.rsqrt(jnp.mean(centre * centre, axis=1, keepdims=True) + EPS)
        normed = centre * inverse
        scaled = upstream * gain
        shift = jnp.mean(scaled, axis=1, keepdims=True)
        tilt = jnp.mean(scaled * normed, axis=1, keepdims=True)
        grad = inverse * (scaled - shift - normed * tilt)
        low[rows, :] = grad.astype(BF16)

        def fold(value):
            return jnp.sum(value.reshape(8, 8, 512), axis=0)

        return (carry[0] + fold(grad), carry[1] + fold(upstream * normed), carry[2] + fold(upstream))

    zero = jnp.zeros((8, 512), F32)
    vectors = lax.fori_loop(0, 8, norm, (zero, zero, zero))
    sums[...] = jnp.zeros((16, 256), F32)
    for i in range(3):
        row = jnp.sum(vectors[i], axis=0, keepdims=True)
        sums[6 + 2 * i : 7 + 2 * i, :] = row[:, 0:256]
        sums[7 + 2 * i : 8 + 2 * i, :] = row[:, 256:512]

    for slot in range(2):
        half = hid if slot == 0 else 1 - hid

        for j in range(3):
            if j < 2:
                rows = slice(256 * j, 256 * j + 256)
                grad = ndot(low[:, 0:256], weights[slot, 0, rows, :]) + ndot(
                    low[:, 256:512], weights[slot, 1, rows, :]
                )
            else:
                grad = ndot(low[:, 0:256], weights[slot, 2, 0:256, :]) + ndot(
                    low[:, 256:512], weights[slot, 2, 256:512, :]
                )
            grad = grad * slope[3 * slot + j]
            sums[pl.ds(3 * half + j, 1), :] = jnp.sum(grad, axis=0, keepdims=True)
            pre_low[3 * slot + j] = grad.astype(BF16)

        for j in range(3):
            part = tdot(act[3 * slot + j], low[...]).astype(BF16)
            if j < 2:
                place_rows(grads, 0, 256 * j, part[:, 0:256], half)
                place_rows(grads, 1, 256 * j, part[:, 256:512], half)
            else:
                place_rows(grads, 2, 0, part[:, 0:256], half)
                place_rows(grads, 2, 256, part[:, 256:512], half)

    for m in range(9):
        for slot in range(2):
            half = hid if slot == 0 else 1 - hid
            part = dot(inpt[m % 3], pre_low[3 * slot + m // 3]).astype(BF16)
            place_rows(grads, 3 + m, 0, part, half)

    for r in range(3):
        total = jnp.zeros((512, 512), F32)
        for slot in range(2):
            for j in range(3):
                total = total + ndot(pre_low[3 * slot + j], weights[slot, 3 + 3 * j + r])
        if r == 0:
            grad_edge_ref[...] = (total + up[...]).astype(BF16)
        elif r == 1:
            table = dot(pick_src[...], total.astype(BF16))
            own_table[...] = table[0:256]
            halo_table[...] = table[256:384].astype(BF16)
        else:
            own_table[...] += dot(pick_dst[...], total.astype(BF16))


def reduce_kernel(
    grads,
    sums,
    own_table,
    halo_table,
    send_ref,
    total,
    grad_node,
    summed,
    core_in,
    stage,
    first_in,
    first_out,
    second_in,
    second_out,
    third_in,
    sum_core,
    sum_ring,
    halo_in,
    node_out,
    node_in,
    reduce_send,
    reduce_recv,
    gather_send,
    gather_recv,
    sum_send,
    sum_recv,
    node_send,
    node_recv,
):
    place = Place()
    core = place.core
    partners = [place.ring(axis, j) for axis in "zxy" for j in RING]
    partners += [place.other_core(), place.partition(1), place.partition(63)]
    ready(partners)
    flying = []

    def go(src, dst, send_sem, recv_sem, target):
        copy = remote(src, dst, send_sem, recv_sem, target)
        copy.start()
        flying.append(copy)
        return copy

    up = go(halo_table.at[64:128], halo_in.at[0], node_send.at[0], node_recv.at[0], place.partition(1))
    down = go(halo_table.at[0:64], halo_in.at[1], node_send.at[1], node_recv.at[1], place.partition(63))
    sum_copy = go(sums, sum_core.at[0], sum_send.at[0, 0], sum_recv.at[0, 0], place.other_core())
    between = {}
    for chunk in range(CHUNKS):
        between[chunk] = go(
            grads.at[2 * chunk + 1 - core],
            core_in.at[chunk],
            reduce_send.at[chunk, 0],
            reduce_recv.at[chunk, 0],
            place.other_core(),
        )

    def spread(chunk, level, src, dst, unit):
        axis = REDUCE_AXES[kind(chunk)][level]
        mine = getattr(place, axis)
        copies = []
        for j in RING:
            at = lax.rem(mine + j, 4)
            sem = 1 + 3 * level + j - 1
            copies.append(
                go(
                    src.at[rows_of(at, 1, unit)],
                    dst.at[j - 1],
                    reduce_send.at[chunk, sem],
                    reduce_recv.at[chunk, sem],
                    place.ring(axis, j),
                )
            )
        return copies

    def kept(chunk, level, src, unit):
        mine = getattr(place, REDUCE_AXES[kind(chunk)][level])
        return src[rows_of(mine, 1, unit), :].astype(F32)

    def add_core(chunk):
        between[chunk].wait_recv()

        def part(i, _):
            rows = pl.ds(pl.multiple_of(i * 128, 128), 128)
            mine = grads[2 * chunk + core, rows, :].astype(F32)
            stage[chunk, rows, :] = (mine + core_in[chunk, rows, :].astype(F32)).astype(BF16)
            return 0

        lax.fori_loop(0, 8, part, 0)

    def sums_ring(level, axis, value):
        mine = getattr(place, axis)
        sum_ring[level, mine] = value
        return [
            go(
                sum_ring.at[level, mine],
                sum_ring.at[level, mine],
                sum_send.at[1 + level, j],
                sum_recv.at[1 + level, j],
                place.ring(axis, j),
            )
            for j in RING
        ]

    waiting = {}
    for chunk in range(CHUNKS):
        add_core(chunk)
        waiting[chunk] = spread(chunk, 0, stage.at[chunk], first_in.at[chunk], 256)
    sum_copy.wait_recv()
    ring_copies = sums_ring(0, "z", sums[...] + sum_core[0])

    up.wait_recv()
    down.wait_recv()
    node = own_table[...]
    for side in (0, 1):
        picks = (lax.broadcasted_iota(jnp.int32, (256, 64), 0) == send_ref[side : side + 1, :]).astype(F32)
        got = halo_in[side]
        there = (place.dom < 63) if side == 1 else (place.dom > 0)
        picks = jnp.where(there, picks, 0.0).astype(BF16)
        node = node + jnp.dot(picks, got, preferred_element_type=F32)
    node_keep = jnp.where(place.hid == 0, node[:, 0:256], node[:, 256:512])
    node_out[...] = jnp.where(place.hid == 0, node[:, 256:512], node[:, 0:256]).astype(BF16)
    swap = go(node_out, node_in, node_send.at[2], node_recv.at[2], (place.dom, 1 - place.hid))

    for chunk in range(CHUNKS):
        for copy in waiting[chunk]:
            copy.wait_recv()
        value = kept(chunk, 0, stage.at[chunk], 256)
        for j in range(3):
            value = value + first_in[chunk, j].astype(F32)
        first_out[chunk] = value.astype(BF16)
        waiting[chunk] = spread(chunk, 1, first_out.at[chunk], second_in.at[chunk], 64)
    for copy in ring_copies:
        copy.wait_recv()
    ring_copies = sums_ring(1, "x", sum_ring[0, 0] + sum_ring[0, 1] + sum_ring[0, 2] + sum_ring[0, 3])
    for chunk in range(CHUNKS):
        for copy in waiting[chunk]:
            copy.wait_recv()
        value = kept(chunk, 1, first_out.at[chunk], 64)
        for j in range(3):
            value = value + second_in[chunk, j].astype(F32)
        second_out[chunk] = value.astype(BF16)
        waiting[chunk] = spread(chunk, 2, second_out.at[chunk], third_in.at[chunk], 16)
    for copy in ring_copies:
        copy.wait_recv()
    ring_copies = sums_ring(2, "y", sum_ring[1, 0] + sum_ring[1, 1] + sum_ring[1, 2] + sum_ring[1, 3])
    gather = Gather(place, total, gather_send, gather_recv)
    for chunk in range(CHUNKS):
        for copy in waiting[chunk]:
            copy.wait_recv()
        value = kept(chunk, 2, second_out.at[chunk], 16)
        for j in range(3):
            value = value + third_in[chunk, j].astype(F32)
        value = value * (1.0 / 1024)
        total[2 * chunk + core, rows_of(own_tile(place, chunk), 1), :] = value.astype(BF16)
        gather.start(chunk, 0)
    swap.wait_recv()
    grad_node[...] = (node_keep + node_in[...].astype(F32)).astype(BF16)
    for step in (1, 2, 3):
        for chunk in range(CHUNKS):
            gather.arrived(chunk, step - 1)
            gather.start(chunk, step)
    for copy in ring_copies:
        copy.wait_recv()
    summed[...] = (sum_ring[2, 0] + sum_ring[2, 1] + sum_ring[2, 2] + sum_ring[2, 3]) * (1.0 / 1024)
    for chunk in range(CHUNKS):
        gather.arrived(chunk, 3)
    gather.sent()
    for copy in flying:
        copy.wait_send()


def widen_kernel(total, w_out, w_in):
    step = pl.program_id(0)

    @pl.when(step == 0)
    def _():
        w_out[0:512, 0:256] = total[0].astype(F32)

    @pl.when(step == 1)
    def _():
        w_out[0:512, 256:512] = total[0].astype(F32)

    @pl.when(step == 2)
    def _():
        w_out[512:768, 0:256] = total[0, 0:256].astype(F32)
        w_out[512:768, 256:512] = total[0, 256:512].astype(F32)

    @pl.when(step >= 3)
    def _():
        w_in[...] = total[0].astype(F32)


def vmem():
    return pl.BlockSpec(memory_space=pltpu.VMEM)


def smem():
    return pl.BlockSpec(memory_space=pltpu.SMEM)


def anywhere():
    return pl.BlockSpec(memory_space=pl.ANY)


def shape(dims, dtype):
    return jax.ShapeDtypeStruct(dims, dtype)


def dma(*dims):
    return pltpu.SemaphoreType.DMA(dims)


def per_device(
    node_latent,
    edge_latent,
    send_rows,
    edge_src,
    edge_dst,
    edge_live,
    w_in_blocks,
    w_in_scale,
    bias_in,
    w_out_blocks,
    w_out_scale,
    bias_out,
    norm_gain,
    grad_edge,
    grad_agg,
):
    lists = send_rows[0]
    weights, bias, halo = pl.pallas_call(
        weights_kernel,
        out_shape=(
            shape((2, 12, 512, 256), BF16),
            shape((2, 8, 256), F32),
            shape((2, 64, 512), BF16),
        ),
        in_specs=[vmem(), smem(), vmem(), smem(), vmem(), vmem(), vmem()],
        out_specs=(vmem(), vmem(), vmem()),
        scratch_shapes=[
            pltpu.VMEM((2, 64, 512), BF16),
            dma(6, 8),
            dma(6, 8),
            dma(7),
            dma(7),
            dma(2),
            dma(2),
        ],
        compiler_params=pltpu.CompilerParams(
            collective_id=0, has_side_effects=True, vmem_limit_bytes=LIMIT
        ),
        name="spread_weights",
    )(w_in_blocks, w_in_scale, w_out_blocks, w_out_scale, bias_in.reshape(3, 256), node_latent, lists)
    grad_edge_in, grads, own_table, halo_table, sums = pl.pallas_call(
        compute_kernel,
        out_shape=(
            shape((512, 512), BF16),
            shape((12, 1024, 256), BF16),
            shape((256, 512), F32),
            shape((128, 512), BF16),
            shape((16, 256), F32),
        ),
        in_specs=[
            anywhere(),
            anywhere(),
            vmem(),
            vmem(),
            vmem(),
            vmem(),
            vmem(),
            smem(),
            vmem(),
            vmem(),
            vmem(),
            vmem(),
        ],
        out_specs=(vmem(),) * 5,
        scratch_shapes=[
            pltpu.VMEM((3, 512, 512), BF16),
            pltpu.VMEM((3, 512, 512), BF16),
            pltpu.VMEM((384, 512), BF16),
            pltpu.VMEM((384, 512), BF16),
            pltpu.VMEM((256, 512), BF16),
            pltpu.VMEM((6, 512, 256), BF16),
            pltpu.VMEM((6, 512, 256), F32),
            pltpu.VMEM((512, 512), F32),
            pltpu.VMEM((512, 512), F32),
            pltpu.VMEM((512, 512), BF16),
            pltpu.VMEM((6, 512, 256), BF16),
            pltpu.VMEM((512, 512), BF16),
            dma(2),
        ],
        compiler_params=pltpu.CompilerParams(vmem_limit_bytes=LIMIT),
        name="local_grads",
    )(
        edge_latent,
        grad_edge,
        node_latent,
        grad_agg,
        halo,
        edge_src.reshape(8, 128),
        edge_dst.reshape(8, 128),
        edge_live,
        weights,
        bias,
        bias_out.reshape(1, 512),
        norm_gain.reshape(1, 512),
    )
    total, grad_node, summed = pl.pallas_call(
        reduce_kernel,
        out_shape=(
            shape((12, 512, 256), BF16),
            shape((256, 256), BF16),
            shape((16, 256), F32),
        ),
        in_specs=[vmem()] * 5,
        out_specs=(vmem(),) * 3,
        scratch_shapes=[
            pltpu.VMEM((6, 1024, 256), BF16),
            pltpu.VMEM((6, 1024, 256), BF16),
            pltpu.VMEM((6, 3, 256, 256), BF16),
            pltpu.VMEM((6, 256, 256), BF16),
            pltpu.VMEM((6, 3, 64, 256), BF16),
            pltpu.VMEM((6, 64, 256), BF16),
            pltpu.VMEM((6, 3, 16, 256), BF16),
            pltpu.VMEM((1, 16, 256), F32),
            pltpu.VMEM((3, 4, 16, 256), F32),
            pltpu.VMEM((2, 64, 512), BF16),
            pltpu.VMEM((256, 256), BF16),
            pltpu.VMEM((256, 256), BF16),
            dma(6, 10),
            dma(6, 10),
            dma(6, 8),
            dma(6, 8),
            dma(4, 4),
            dma(4, 4),
            dma(3),
            dma(3),
        ],
        compiler_params=pltpu.CompilerParams(
            collective_id=1, has_side_effects=True, vmem_limit_bytes=LIMIT
        ),
        name="reduce_grads",
    )(grads, sums, own_table, halo_table, lists)
    grad_w_out, grad_w_in = pl.pallas_call(
        widen_kernel,
        grid=(12,),
        out_shape=(shape((768, 512), F32), shape((1536, 768), F32)),
        in_specs=[pl.BlockSpec((1, 512, 256), lambda i: (i, 0, 0))],
        out_specs=(
            pl.BlockSpec((768, 512), lambda i: (0, 0)),
            pl.BlockSpec(
                (512, 256), lambda i: (jnp.maximum(i - 3, 0) % 3, jnp.maximum(i - 3, 0) // 3)
            ),
        ),
        name="widen_grads",
    )(total)
    hid = lax.axis_index("hid")
    grad_bias = jnp.where(hid == 0, summed[0:3], summed[3:6]).reshape(768)
    vectors = summed[6:12].reshape(3, 512)
    return (grad_edge_in, grad_node, grad_w_in, grad_bias, grad_w_out, vectors)


def solution(mesh):
    in_specs = (
        P("dom", None),
        P("dom", None),
        P("dom", None, None),
        P("dom"),
        P("dom"),
        P("dom"),
        P(None, "hid"),
        P(None, "hid"),
        P("hid"),
        P("hid", None),
        P("hid", None),
        P(),
        P(),
        P("dom", None),
        P("dom", None),
    )
    out_specs = (
        P(("dom", "hid"), None),
        P("dom", "hid"),
        P(None, "hid"),
        P("hid"),
        P("hid", None),
        P(),
    )
    return jax.shard_map(
        per_device, mesh=mesh, in_specs=in_specs, out_specs=out_specs, check_vma=False
    )
```

time: 827 us -> 123 us (0.15)
  waiting for transfers between devices: 449 us -> 0 us
  blocking collectives: 273 us -> 0 us
  Pallas kernels: 0 us -> 113 us
  matrix products: 25.9 us -> 0 us
  local copies, waits for them, and re-layouts: 32.9 us -> 7.5 us
  other arithmetic: 17.8 us -> 0.78 us
  between operations: 14.9 us -> 1.31 us
  starting transfers between devices: 12.4 us -> 0 us
    psum x2 -> x0, waiting for transfers between devices: 358 us -> none  [the longest x1 287 us: per_device(): lax.psum((grad_w_first, grad_bias_local, grad_w_second, vectors), 'dom')]
    psum x1 -> x0, blocking collectives: 273 us -> none  [per_device(): lax.psum((grad_w_first, grad_bias_local, grad_w_second, vectors), 'dom')]
    pallas_call x0 -> x4, Pallas kernels: none -> 113 us  [the longest x1 50.6 us: per_device(): pl.pallas_call(reduce_kernel, out_shape=(shape((12, 512, 256), BF16), sha...]
    reduce_scatter x2 -> x0, waiting for transfers between devices: 91.6 us -> none  [the longest x1 79.9 us: per_device(): lax.psum_scatter(contract_cols(grad_pre_low, w_first), 'hid', scatter_dim...]
    dot_general x7 -> x0, matrix products: 25.9 us -> none  [the longest x2 8.46 us: contract_rows(): lax.dot_general(left_side, right_side, (((0,), (0,)), ((), ())), preferre...]
    gather x5 -> x0, local copies, waits for them, and re-layouts: 15.3 us -> none  [the longest x1 3.97 us: per_device(): jnp.take(grad_agg, edge_dst, axis=0).astype(jnp.float32)]
    ppermute x4 -> x0, starting transfers between devices: 12.1 us -> none  [passed_along(): return lax.ppermute(block, axis, route)]
    unnamed x64 -> x3, local copies, waits for them, and re-layouts: 15.5 us -> 4.29 us
  transfers between devices with their start and end apart: 8 -> 0, of which waited for: 4 -> 0; matrix products, arithmetic and copies ran while one was open for 4% -> 0% of each run, Pallas kernels for 0% -> 0%
where the time goes in v1:
time: 123 us; the launch traced here: 122 us
  Pallas kernels  113 us (92%)
  local copies, waits for them, and re-layouts  7.5 us (6%)
  between operations  1.31 us (1%)
    pallas_call x1, Pallas kernels, per_device(): pl.pallas_call(reduce_kernel, out_shape=(shape((12, 512, 256), BF16), sha...  50.6 us
    pallas_call x1, Pallas kernels, per_device(): pl.pallas_call(weights_kernel, out_shape=(shape((2, 12, 512, 256), BF16),...  33.4 us
    pallas_call x1, Pallas kernels, per_device(): pl.pallas_call(compute_kernel, out_shape=(shape((512, 512), BF16), shape(...  19.9 us
    pallas_call x1, Pallas kernels, per_device(): pl.pallas_call(widen_kernel, grid=(12,), out_shape=(shape((768, 512), F32...  8.64 us
    unnamed x3, local copies, waits for them, and re-layouts  4.29 us

profile of v1, /device:TPU:1, one launch (start us, length us, event | category | flops | bytes accessed | tf_op | source)
XLA Modules:
  0.0 122.1 jit_solution(12012770149788741411)
XLA Ops:
  0.6 1.4 %copy.21.w_in_scale = f32[12,6]{1,0:T(8,128)} copy(f32[12,6]{0,1:T(8,128)} %param.22) | data formatting | bytes 576 | tf_op args[7]
  2.0 1.4 %copy.22.w_out_scale = f32[6,4]{1,0:T(8,128)} copy(f32[6,4]{0,1:T(4,128)} %param.25) | data formatting | bytes 192 | tf_op args[10]
  3.4 1.3 %reshape.33.bias_ref = f32[3,256]{1,0:T(4,128)} reshape(f32[768]{0:T(1024)} %param.23) | data formatting | bytes 6144 | tf_op jit(solution)/shard_map/reshape | solution.py:683
  4.6 33.4 %spread_weights.1 = (bf16[2,12,512,256]{3,2,1,0:T(8,128)(2,1)}, f32[2,8,256]{2,1,0:T(8,128)}, bf16[2,64,512]{2,1,0:T(8,128)(2,1)}) custom-call(bf16[1536,768]{1,0:T(8,128)(2,1)} %w_in_ref.1, f32[12,6]{1,0:T(8,128)} %copy.21.w_in_scale, bf16[768,512]{1,0:T(8,128)(2,1)} %w_out_ref.1, f32[6,4]{1,0:T(8,128)} %copy.22.w_out_scale, f32[3,256]{1,0:T(4,128)} %reshape.33.bias_ref, ...), custom_call_target="tpu_custom_call" | custom-call | tf_op jit(solution)/shard_map/spread_weights/pallas_call | solution.py:661
  38.7 19.9 %local_grads.1 = (bf16[512,512]{1,0:T(8,128)(2,1)}, bf16[12,1024,256]{2,1,0:T(8,128)(2,1)}, f32[256,512]{1,0:T(8,128)}, bf16[128,512]{1,0:T(8,128)(2,1)}, f32[16,256]{1,0:T(8,128)}) custom-call(bf16[1024,512]{1,0:T(8,128)(2,1)} %edge_ref.1, bf16[1024,512]{1,0:T(8,128)(2,1)} %gedge_ref.1, bf16[256,512]{1,0:T(8,128)(2,1)} %node_ref.3, ...), custom_call_target="tpu_custom_call" | custom-call | tf_op jit(solution)/shard_map/local_grads/pallas_call | solution.py:684
  58.6 50.6 %reduce_grads.1 = (bf16[12,512,256]{2,1,0:T(8,128)(2,1)}, bf16[256,256]{1,0:T(8,128)(2,1)}, f32[16,256]{1,0:T(8,128)}) custom-call(bf16[12,1024,256]{2,1,0:T(8,128)(2,1)} %get-tuple-element.23.grads, f32[16,256]{1,0:T(8,128)} %get-tuple-element.24.sums, f32[256,512]{1,0:T(8,128)} %get-tuple-element.25.own_table, ...), custom_call_target="tpu_custom_call" | custom-call | tf_op jit(solution)/shard_map/reduce_grads/pallas_call | solution.py:739
  109.2 8.6 %widen_grads.1 = (f32[768,512]{1,0:T(8,128)}, f32[1536,768]{1,0:T(8,128)}) custom-call(bf16[12,512,256]{2,1,0:T(8,128)(2,1)} %get-tuple-element.28.total), custom_call_target="tpu_custom_call" | custom-call | tf_op jit(solution)/shard_map/widen_grads/pallas_call | solution.py:775
  117.9 0.7 slice.11
  118.6 0.6 reshape.39
  119.2 0.8 slice_select_fusion
  120.0 0.6 reshape.38
  120.6 1.6 %copy.25 = bf16[256,256]{1,0:T(8,128)(2,1)} copy(bf16[256,256]{1,0:T(8,128)(2,1)} %get-tuple-element.39) | data formatting | bytes 262144

commit v2 on v0

v2 whole, which is shorter than its diff:
```python
import jax
import jax.numpy as jnp
from jax import lax
from jax.experimental import pallas as pl
from jax.experimental.pallas import tpu as pltpu
from jax.sharding import PartitionSpec as P

EPS = 1e-05
MESH = pl.DeviceIdType.MESH
F32 = jnp.float32
BF16 = jnp.bfloat16
CHUNKS = 6
LIMIT = 60 << 20


class Place:
    def __init__(self):
        dom = lax.axis_index("dom")
        self.hid = lax.axis_index("hid")
        self.dom = dom
        self.z = lax.div(dom, 16)
        self.x = lax.rem(lax.div(dom, 4), 4)
        self.yl = lax.rem(lax.div(dom, 2), 2)
        self.y = 2 * self.hid + self.yl
        self.core = lax.rem(dom, 2)

    def at(self, z=None, x=None, y=None, core=None):
        z = self.z if z is None else z
        x = self.x if x is None else x
        y = self.y if y is None else y
        core = self.core if core is None else core
        return (((z * 4 + x) * 2 + lax.rem(y, 2)) * 2 + core, lax.div(y, 2))

    def ring(self, axis, step):
        return self.at(**{axis: lax.rem(getattr(self, axis) + step, 4)})

    def other_core(self):
        return self.at(core=1 - self.core)

    def cross(self):
        return self.at(y=3 - self.y)

    def pair(self):
        return self.at(y=self.y + 1 - 2 * self.yl)

    def partition(self, step):
        return (lax.rem(self.dom + step, 64), self.hid)


def greet(partners):
    barrier = pltpu.get_barrier_semaphore()
    for partner in partners:
        pl.semaphore_signal(barrier, inc=1, device_id=partner, device_id_type=MESH)
    return lambda: pl.semaphore_wait(barrier, len(partners))


def remote(src, dst, send_sem, recv_sem, target):
    return pltpu.make_async_remote_copy(
        src_ref=src,
        dst_ref=dst,
        send_sem=send_sem,
        recv_sem=recv_sem,
        device_id=target,
        device_id_type=MESH,
    )


def kind(chunk):
    return chunk % 3


def own_tile(place, chunk, yl=None):
    yl = place.yl if yl is None else yl
    if kind(chunk) == 0:
        return (place.z * 4 + place.x) * 2 + yl
    if kind(chunk) == 1:
        return (place.x * 2 + yl) * 4 + place.z
    return (yl * 4 + place.z) * 4 + place.x


def rows_of(first, count, unit=16):
    return pl.ds(pl.multiple_of(first * unit, unit), count * unit)


def gather_steps(place, chunk):
    z, x, yl = place.z, place.x, place.yl
    z_ring = [place.ring("z", j) for j in (1, 2, 3)]
    x_ring = [place.ring("x", j) for j in (1, 2, 3)]
    pair = [place.pair()]
    if kind(chunk) == 0:
        return [
            ((z * 4 + x) * 2 + yl, 1, pair),
            ((z * 4 + x) * 2, 2, x_ring),
            (z * 8, 8, z_ring),
        ]
    if kind(chunk) == 1:
        return [
            ((x * 2 + yl) * 4 + z, 1, z_ring),
            ((x * 2 + yl) * 4, 4, pair),
            (x * 8, 8, x_ring),
        ]
    return [
        ((yl * 4 + z) * 4 + x, 1, x_ring),
        ((yl * 4 + z) * 4, 4, z_ring),
        (yl * 16, 16, pair),
    ]


class Gather:
    def __init__(self, place, buf, send_sem, recv_sem, result):
        self.place, self.buf, self.result = place, buf, result
        self.send_sem, self.recv_sem = send_sem, recv_sem
        self.steps = {}
        self.flying = {}

    def start(self, chunk, step):
        place = self.place
        if chunk not in self.steps:
            self.steps[chunk] = gather_steps(place, chunk)
        block = 2 * chunk + place.core
        if step == 3:
            first, count, targets = 0, 32, [place.other_core()]
            base = 7
        else:
            first, count, targets = self.steps[chunk][step]
            base = sum(len(s[2]) for s in self.steps[chunk][:step])
        part = self.buf.at[block, rows_of(first, count)]
        goal = self.result.at[block] if step == 3 else part
        copies = []
        for j, target in enumerate(targets):
            copy = remote(
                part, goal, self.send_sem.at[chunk, base + j], self.recv_sem.at[chunk, base + j], target
            )
            copy.start()
            copies.append(copy)
        self.flying[chunk, step] = copies

    def arrived(self, chunk, step):
        for copy in self.flying[chunk, step]:
            copy.wait_recv()

    def sent(self):
        for copies in self.flying.values():
            for copy in copies:
                copy.wait_send()


RING = (1, 2, 3)
REDUCE_AXES = {0: ("z", "x", "y"), 1: ("x", "y", "z"), 2: ("y", "z", "x")}


def tdot(a, b):
    return lax.dot_general(a, b, (((0,), (0,)), ((), ())), preferred_element_type=F32)


def ndot(a, b):
    return lax.dot_general(a, b, (((1,), (1,)), ((), ())), preferred_element_type=F32)


def dot(a, b):
    return jnp.dot(a, b, preferred_element_type=F32)


def dequantize_out(own, w_out_ref, scales):
    for a in range(6):
        for b in range(4):
            value = w_out_ref[128 * a : 128 * a + 128, 128 * b : 128 * b + 128].astype(F32) * scales[b, a]
            if a < 4:
                index, row = b // 2, 128 * a
            else:
                index, row = 2, 128 * (a - 4) + 256 * (b // 2)
            col = 128 * (b % 2)
            own[index, row : row + 128, col : col + 128] = value.astype(BF16)


def dequantize_in(own, w_in_ref, scales, first, last):
    def block(index, _):
        j = lax.div(index, 3)
        r = lax.rem(index, 3)
        for a in range(4):
            for b in range(2):
                scale = scales[2 * j + b, 4 * r + a]
                rows = pl.ds(pl.multiple_of(512 * r + 128 * a, 128), 128)
                cols = pl.ds(pl.multiple_of(256 * j + 128 * b, 128), 128)
                value = w_in_ref[rows, cols].astype(F32) * scale
                own[3 + index, 128 * a : 128 * a + 128, 128 * b : 128 * b + 128] = value.astype(BF16)
        return 0

    lax.fori_loop(first, last, block, 0)


def dequantize_tile(tile, w_in_ref, scales, index, q):
    j = lax.div(index, 3)
    r = lax.rem(index, 3)
    rows = pl.ds(pl.multiple_of(512 * r + 16 * q, 16), 16)
    for b in range(2):
        scale = scales[2 * j + b, 4 * r + lax.div(q, 8)]
        cols = pl.ds(pl.multiple_of(256 * j + 128 * b, 128), 128)
        tile[:, 128 * b : 128 * b + 128] = (w_in_ref[rows, cols].astype(F32) * scale).astype(BF16)


def place_rows(grads, block, first, value, half):
    count = value.shape[0]
    group = {0: 32, 1: 128, 2: 512}[kind(block // 2)]
    size = min(group, count)
    for at in range(0, count, size):
        row = first + at
        base = (row // group) * 2 * group + row % group
        grads[block, pl.ds(pl.multiple_of(base + group * half, 32), size), :] = value[at : at + size]


class Reduce:
    def __init__(self, place, grads, core_in, first_in, first_out, second_in, second_out, third_in, send_sem, recv_sem):
        self.place, self.grads, self.core_in = place, grads, core_in
        self.first_in, self.first_out = first_in, first_out
        self.second_in, self.second_out, self.third_in = second_in, second_out, third_in
        self.send_sem, self.recv_sem = send_sem, recv_sem
        self.flying = {}

    def send(self, chunk, stage, index, src, dst, target):
        copy = remote(src, dst, self.send_sem.at[chunk, index], self.recv_sem.at[chunk, index], target)
        copy.start()
        self.flying.setdefault((chunk, stage), []).append(copy)

    def arrived(self, chunk, stage):
        for copy in self.flying[chunk, stage]:
            copy.wait_recv()

    def sent(self):
        for copies in self.flying.values():
            for copy in copies:
                copy.wait_send()

    def share(self, chunk):
        core = self.place.core
        src = self.grads.at[2 * chunk + 1 - core]
        self.send(chunk, 0, 0, src, self.core_in.at[chunk], self.place.other_core())

    def spread(self, chunk, level, src, dst, unit):
        axis = REDUCE_AXES[kind(chunk)][level]
        mine = getattr(self.place, axis)
        for j in RING:
            at = lax.rem(mine + j, 4)
            part = src.at[rows_of(at, 1, unit)]
            self.send(chunk, level + 1, 3 * level + j, part, dst.at[j - 1], self.place.ring(axis, j))

    def kept(self, chunk, level, src, unit):
        mine = getattr(self.place, REDUCE_AXES[kind(chunk)][level])
        return src[rows_of(mine, 1, unit), :].astype(F32)

    def add_core(self, chunk):
        self.arrived(chunk, 0)
        block = 2 * chunk + self.place.core

        def part(i, _):
            rows = pl.ds(pl.multiple_of(i * 128, 128), 128)
            mine = self.grads[block, rows, :].astype(F32)
            self.grads[block, rows, :] = (mine + self.core_in[chunk, rows, :].astype(F32)).astype(BF16)
            return 0

        lax.fori_loop(0, 8, part, 0)
        self.spread(chunk, 0, self.grads.at[block], self.first_in.at[chunk], 256)

    def add_first(self, chunk):
        self.arrived(chunk, 1)
        value = self.kept(chunk, 0, self.grads.at[2 * chunk + self.place.core], 256)
        for j in range(3):
            value = value + self.first_in[chunk, j].astype(F32)
        self.first_out[chunk] = value.astype(BF16)
        self.spread(chunk, 1, self.first_out.at[chunk], self.second_in.at[chunk], 64)

    def add_second(self, chunk):
        self.arrived(chunk, 2)
        value = self.kept(chunk, 1, self.first_out.at[chunk], 64)
        for j in range(3):
            value = value + self.second_in[chunk, j].astype(F32)
        self.second_out[chunk] = value.astype(BF16)
        self.spread(chunk, 2, self.second_out.at[chunk], self.third_in.at[chunk], 16)

    def add_third(self, chunk):
        self.arrived(chunk, 3)
        value = self.kept(chunk, 2, self.second_out.at[chunk], 16)
        for j in range(3):
            value = value + self.third_in[chunk, j].astype(F32)
        return value


def main_kernel(
    node_hbm,
    edge_hbm,
    send_ref,
    src_ref,
    dst_ref,
    live_ref,
    w_in_hbm,
    w_in_scale,
    bias_ref,
    w_out_hbm,
    w_out_scale,
    bias_out_ref,
    gain_ref,
    gedge_hbm,
    gagg_hbm,
    total_hbm,
    grad_edge,
    grad_node,
    summed,
    node,
    w_in,
    w_out,
    gagg,
    gedge,
    weights,
    bias,
    halo,
    halo_out,
    tiles,
    inp,
    inpt,
    ext,
    pick_src,
    pick_dst,
    act,
    slope,
    up,
    msg,
    low,
    pre_low,
    grads,
    core_in,
    first_in,
    first_out,
    second_in,
    second_out,
    third_in,
    total,
    sums,
    sum_core,
    sum_ring,
    own_table,
    halo_table,
    halo_in,
    node_out,
    node_in,
    local_sem,
    spread_send,
    spread_recv,
    cross_send,
    cross_recv,
    halo_send,
    halo_recv,
    reduce_send,
    reduce_recv,
    gather_send,
    gather_recv,
    sum_send,
    sum_recv,
    node_send,
    node_recv,
    write_sem,
):
    place = Place()
    hid, dom, core = place.hid, place.dom, place.core
    first_edge = pl.multiple_of(hid * 512, 512)

    def fetch(index, src, dst):
        copy = pltpu.make_async_copy(src, dst, local_sem.at[index])
        copy.start()
        return copy

    get_w_in = fetch(1, w_in_hbm, w_in)
    get_w_out = fetch(0, w_out_hbm, w_out)
    get_node = fetch(2, node_hbm, node)
    get_edge = fetch(3, edge_hbm.at[pl.ds(first_edge, 512)], inp.at[0])
    get_agg = fetch(4, gagg_hbm, gagg)
    get_cot = fetch(5, gedge_hbm.at[pl.ds(first_edge, 512)], gedge)
    partners = [place.ring(axis, j) for axis in "zxy" for j in RING]
    partners += [place.other_core(), place.cross(), place.partition(1), place.partition(63)]
    all_here = greet(partners)
    flying = []

    def go(src, dst, send_sem, recv_sem, target):
        copy = remote(src, dst, send_sem, recv_sem, target)
        copy.start()
        flying.append(copy)
        return copy

    own, other = weights.at[0], weights.at[1]
    bias[0] = jnp.zeros((8, 256), F32)
    for j in range(3):
        bias[0, j : j + 1, 0:128] = bias_ref[2 * j : 2 * j + 1, :]
        bias[0, j : j + 1, 128:256] = bias_ref[2 * j + 1 : 2 * j + 2, :]
    get_w_in.wait()
    tile_at = {}
    for chunk in (2, 3, 4, 5):
        tile_at[chunk] = own_tile(place, chunk, 1 - place.yl)
        dequantize_tile(tiles.at[chunk - 2], w_in, w_in_scale, 2 * chunk + core - 3, tile_at[chunk])
    dequantize_in(own, w_in, w_in_scale, 0, 1)
    get_w_out.wait()
    dequantize_out(own, w_out, w_out_scale)
    all_here()
    crossing = {}
    for chunk in (2, 3, 4, 5, 1, 0):
        block = 2 * chunk + core
        if chunk < 2:
            src, dst = own.at[block], other.at[block]
        else:
            src, dst = tiles.at[chunk - 2], other.at[block, rows_of(tile_at[chunk], 1)]
        crossing[chunk] = go(src, dst, cross_send.at[chunk], cross_recv.at[chunk], place.cross())
    bias_copy = go(bias.at[0], bias.at[1], cross_send.at[6], cross_recv.at[6], place.cross())
    get_node.wait()
    for side in (0, 1):
        picks = (lax.broadcasted_iota(jnp.int32, (256, 64), 0) == send_ref[side : side + 1, :]).astype(F32)
        halo_out[side] = tdot(picks.astype(BF16), node[...]).astype(BF16)
    up_rows = go(halo_out.at[1], halo.at[0], halo_send.at[0], halo_recv.at[0], place.partition(1))
    down_rows = go(halo_out.at[0], halo.at[1], halo_send.at[1], halo_recv.at[1], place.partition(63))
    for k in range(4):
        cols = slice(128 * k, 128 * k + 128)
        src_row = src_ref[pl.ds(4 * hid + k, 1), :]
        dst_row = dst_ref[pl.ds(4 * hid + k, 1), :]
        pick_src[:, cols] = (lax.broadcasted_iota(jnp.int32, (384, 128), 0) == src_row).astype(F32).astype(BF16)
        pick_dst[:, cols] = (lax.broadcasted_iota(jnp.int32, (256, 128), 0) == dst_row).astype(F32).astype(BF16)
    spread = Gather(place, other, spread_send, spread_recv, other)
    for chunk in (2, 3, 4, 5):
        crossing[chunk].wait_recv()
        spread.start(chunk, 0)
    dequantize_in(own, w_in, w_in_scale, 1, 9)
    for chunk in (2, 3, 4, 5):
        spread.arrived(chunk, 0)
        spread.start(chunk, 1)
    inp[2] = tdot(pick_dst[...], node[...]).astype(BF16)
    get_agg.wait()
    up[...] = tdot(pick_dst[...], gagg[...])
    ext[0:256] = node[...]
    up_rows.wait_recv()
    down_rows.wait_recv()
    ext[256:320] = jnp.where(dom > 0, halo[0], jnp.zeros((64, 512), BF16))
    ext[320:384] = jnp.where(dom < 63, halo[1], jnp.zeros((64, 512), BF16))
    inp[1] = tdot(pick_src[...], ext[...]).astype(BF16)
    get_edge.wait()
    for chunk in (2, 3, 4, 5):
        spread.arrived(chunk, 1)
        spread.start(chunk, 2)

    def forward(slot, j):
        pre = bias[slot, pl.ds(j, 1), :]
        for r in range(3):
            pre = pre + dot(inp[r], weights[slot, 3 + 3 * j + r])
        sigma = 1.0 / (1.0 + jnp.exp(-pre))
        value = pre * sigma
        act[3 * slot + j] = value.astype(BF16)
        slope[3 * slot + j] = sigma + value * (1.0 - sigma)

    def forward_own(j, _):
        forward(0, j)
        return 0

    lax.fori_loop(0, 3, forward_own, 0)
    crossing[1].wait_recv()
    spread.start(1, 3)
    for chunk in (2, 3, 4, 5):
        spread.arrived(chunk, 2)
        spread.start(chunk, 3)
    crossing[0].wait_recv()
    spread.start(0, 3)
    for r in range(3):
        inpt[r] = inp[r].T
    get_cot.wait()
    bias_copy.wait_recv()
    for chunk in (1, 2):
        spread.arrived(chunk, 3)
    forward(1, 0)
    for chunk in (3, 4):
        spread.arrived(chunk, 3)
    forward(1, 1)
    spread.arrived(5, 3)
    forward(1, 2)
    spread.arrived(0, 3)

    for side in range(2):
        result = bias_out_ref[:, 256 * side : 256 * side + 256]
        for slot in range(2):
            for j in range(2):
                result = result + dot(act[3 * slot + j], weights[slot, side, 256 * j : 256 * j + 256, :])
            result = result + dot(act[3 * slot + 2], weights[slot, 2, 256 * side : 256 * side + 256, :])
        msg[:, 256 * side : 256 * side + 256] = result

    live = live_ref[0] - hid * 512
    gain = gain_ref[...]

    def norm(i, carry):
        rows = pl.ds(pl.multiple_of(i * 64, 64), 64)
        mask = (lax.broadcasted_iota(jnp.int32, (64, 512), 0) + i * 64) < live
        upstream = jnp.where(mask, gedge[rows, :].astype(F32) + up[rows, :], 0.0)
        up[rows, :] = upstream
        message = msg[rows, :]
        centre = message - jnp.mean(message, axis=1, keepdims=True)
        inverse = lax.rsqrt(jnp.mean(centre * centre, axis=1, keepdims=True) + EPS)
        normed = centre * inverse
        scaled = upstream * gain
        shift = jnp.mean(scaled, axis=1, keepdims=True)
        tilt = jnp.mean(scaled * normed, axis=1, keepdims=True)
        grad = inverse * (scaled - shift - normed * tilt)
        low[rows, :] = grad.astype(BF16)

        def fold(value):
            return jnp.sum(value.reshape(8, 8, 512), axis=0)

        return (carry[0] + fold(grad), carry[1] + fold(upstream * normed), carry[2] + fold(upstream))

    zero = jnp.zeros((8, 512), F32)
    vectors = lax.fori_loop(0, 8, norm, (zero, zero, zero))
    sums[...] = jnp.zeros((16, 256), F32)
    for i in range(3):
        row = jnp.sum(vectors[i], axis=0, keepdims=True)
        sums[6 + 2 * i : 7 + 2 * i, :] = row[:, 0:256]
        sums[7 + 2 * i : 8 + 2 * i, :] = row[:, 256:512]

    reduce = Reduce(
        place, grads, core_in, first_in, first_out, second_in, second_out, third_in, reduce_send, reduce_recv
    )
    gather = Gather(place, total, gather_send, gather_recv, total_hbm)
    halves = (hid, 1 - hid)
    for slot in range(2):
        for j in range(3):
            part = tdot(act[3 * slot + j], low[...]).astype(BF16)
            if j < 2:
                place_rows(grads, 0, 256 * j, part[:, 0:256], halves[slot])
                place_rows(grads, 1, 256 * j, part[:, 256:512], halves[slot])
            else:
                place_rows(grads, 2, 0, part[:, 0:256], halves[slot])
                place_rows(grads, 2, 256, part[:, 256:512], halves[slot])
    reduce.share(0)
    for slot in range(2):
        for j in range(3):
            if j < 2:
                rows = slice(256 * j, 256 * j + 256)
                grad = ndot(low[:, 0:256], weights[slot, 0, rows, :])
                grad = grad + ndot(low[:, 256:512], weights[slot, 1, rows, :])
            else:
                grad = ndot(low[:, 0:256], weights[slot, 2, 0:256, :])
                grad = grad + ndot(low[:, 256:512], weights[slot, 2, 256:512, :])
            grad = grad * slope[3 * slot + j]
            sums[pl.ds(3 * halves[slot] + j, 1), :] = jnp.sum(grad, axis=0, keepdims=True)
            pre_low[3 * slot + j] = grad.astype(BF16)
    sum_copy = go(sums, sum_core.at[0], sum_send.at[0, 0], sum_recv.at[0, 0], place.other_core())

    def first_layer(m):
        for slot in range(2):
            part = dot(inpt[m % 3], pre_low[3 * slot + m // 3]).astype(BF16)
            place_rows(grads, 3 + m, 0, part, halves[slot])

    def produce(chunk):
        if chunk > 1:
            first_layer(2 * chunk - 3)
        first_layer(2 * chunk - 2)
        reduce.share(chunk)

    def input_grads(r):
        result = jnp.zeros((512, 512), F32)
        for slot in range(2):
            for j in range(3):
                result = result + ndot(pre_low[3 * slot + j], weights[slot, 3 + 3 * j + r])
        return result

    ring_copies = []

    def sums_ring(level, value):
        axis = "zxy"[level]
        mine = getattr(place, axis)
        sum_ring[level, mine] = value
        ring_copies.clear()
        for j in RING:
            part = sum_ring.at[level, mine]
            ring_copies.append(
                go(part, part, sum_send.at[1 + level, j], sum_recv.at[1 + level, j], place.ring(axis, j))
            )

    def ring_sum(level):
        for copy in ring_copies:
            copy.wait_recv()
        return sum_ring[level, 0] + sum_ring[level, 1] + sum_ring[level, 2] + sum_ring[level, 3]

    def extra_a():
        table = dot(pick_src[...], input_grads(1).astype(BF16))
        own_table[...] = table[0:256]
        halo_table[...] = table[256:384].astype(BF16)
        extra["up"] = go(halo_table.at[64:128], halo_in.at[0], node_send.at[0], node_recv.at[0], place.partition(1))
        extra["down"] = go(halo_table.at[0:64], halo_in.at[1], node_send.at[1], node_recv.at[1], place.partition(63))
        sum_copy.wait_recv()
        sums_ring(0, sums[...] + sum_core[0])

    def extra_b():
        own_table[...] += dot(pick_dst[...], input_grads(2).astype(BF16))

    def extra_c():
        grad_edge[...] = (input_grads(0) + up[...]).astype(BF16)

    def extra_d():
        extra["up"].wait_recv()
        extra["down"].wait_recv()
        value = own_table[...]
        for side in (0, 1):
            picks = (lax.broadcasted_iota(jnp.int32, (256, 64), 0) == send_ref[side : side + 1, :]).astype(F32)
            there = (dom < 63) if side == 1 else (dom > 0)
            picks = jnp.where(there, picks, 0.0).astype(BF16)
            value = value + dot(picks, halo_in[side])
        own_table[...] = value
        node_out[...] = jnp.where(hid == 0, value[:, 256:512], value[:, 0:256]).astype(BF16)
        extra["swap"] = go(node_out, node_in, node_send.at[2], node_recv.at[2], (dom, 1 - hid))
        sums_ring(1, ring_sum(0))

    def extra_e():
        sums_ring(2, ring_sum(1))

    def extra_f():
        extra["swap"].wait_recv()
        keep = jnp.where(hid == 0, own_table[:, 0:256], own_table[:, 256:512])
        grad_node[...] = (keep + node_in[...].astype(F32)).astype(BF16)
        summed[...] = ring_sum(2) * (1.0 / 1024)

    extra = {}
    writes = []

    def write(chunk):
        block = 2 * chunk + core
        copy = pltpu.make_async_copy(total.at[block], total_hbm.at[block], write_sem.at[chunk])
        copy.start()
        writes.append(copy)

    def stage(name, chunk):
        if name == "add":
            reduce.add_core(chunk)
        elif name == "first":
            reduce.add_first(chunk)
        elif name == "second":
            reduce.add_second(chunk)
        elif name == "third":
            value = reduce.add_third(chunk) * (1.0 / 1024)
            total[2 * chunk + core, rows_of(own_tile(place, chunk), 1), :] = value.astype(BF16)
            gather.start(chunk, 0)
        elif name == "gather":
            gather.arrived(chunk, 0)
            gather.start(chunk, 1)
        elif name == "more":
            gather.arrived(chunk, 1)
            gather.start(chunk, 2)
        else:
            gather.arrived(chunk, 2)
            gather.start(chunk, 3)
            write(chunk)

    produce(1)
    stage("add", 0)
    produce(2)
    stage("add", 1)
    produce(3)
    stage("add", 2)
    produce(4)
    stage("add", 3)
    produce(5)
    events = []
    for name, chunk_at in (("add", 2.0), ("first", 9.0), ("second", 13.5), ("third", 17.5)):
        for chunk in range(CHUNKS):
            if name != "add" or chunk > 3:
                events.append((chunk_at + 2.0 * chunk, name, chunk))
    for name, chunk_at in (("gather", 21.5), ("more", 25.5), ("last", 31.5)):
        for chunk in range(CHUNKS):
            events.append((chunk_at + 2.0 * chunk, name, chunk))
    for extra_at, run in ((8.5, extra_a), (10.2, extra_b), (11.2, extra_c), (14.4, extra_d), (19.0, extra_e), (25.0, extra_f)):
        events.append((extra_at, "run", run))
    for _, name, item in sorted(events, key=lambda event: event[0]):
        if name == "run":
            item()
        else:
            stage(name, item)
    for chunk in range(CHUNKS):
        gather.arrived(chunk, 3)
    spread.sent()
    reduce.sent()
    gather.sent()
    for copy in flying:
        copy.wait_send()
    for copy in writes:
        copy.wait()


def finish_kernel(
    total, edge_in, node_in, summed, w_out, w_in, bias, vectors, grad_edge, grad_node, raw, wide, read_sem, write_sem
):
    hid = lax.axis_index("hid")
    moves = [
        pltpu.make_async_copy(total.at[block], raw.at[block], read_sem.at[block]) for block in range(12)
    ]
    for copy in moves:
        copy.start()
    through = [
        pltpu.make_async_copy(edge_in, grad_edge, read_sem.at[12]),
        pltpu.make_async_copy(node_in, grad_node, read_sem.at[13]),
    ]
    for copy in through:
        copy.start()
    for i in range(3):
        vectors[i : i + 1, 0:256] = summed[6 + 2 * i : 7 + 2 * i, :]
        vectors[i : i + 1, 256:512] = summed[7 + 2 * i : 8 + 2 * i, :]
    picked = jnp.where(hid == 0, summed[0:3, :], summed[3:6, :])
    for j in range(3):
        for k in range(2):
            bias[2 * j + k : 2 * j + k + 1, :] = picked[j : j + 1, 128 * k : 128 * k + 128]
    writes = []
    for block in range(12):
        moves[block].wait()

        def part(i, _):
            rows = pl.ds(pl.multiple_of(i * 128, 128), 128)
            wide[block, rows, :] = raw[block, rows, :].astype(F32)
            return 0

        lax.fori_loop(0, 4, part, 0)
        if block < 2:
            parts = [(wide.at[block], w_out.at[0:512, 256 * block : 256 * block + 256])]
        elif block == 2:
            parts = [
                (wide.at[2, 0:256], w_out.at[512:768, 0:256]),
                (wide.at[2, 256:512], w_out.at[512:768, 256:512]),
            ]
        else:
            r, j = (block - 3) % 3, (block - 3) // 3
            parts = [(wide.at[block], w_in.at[512 * r : 512 * r + 512, 256 * j : 256 * j + 256])]
        for src, dst in parts:
            copy = pltpu.make_async_copy(src, dst, write_sem.at[len(writes)])
            copy.start()
            writes.append(copy)
    for copy in writes + through:
        copy.wait()


def vmem():
    return pl.BlockSpec(memory_space=pltpu.VMEM)


def smem():
    return pl.BlockSpec(memory_space=pltpu.SMEM)


def anywhere():
    return pl.BlockSpec(memory_space=pl.ANY)


def shape(dims, dtype):
    return jax.ShapeDtypeStruct(dims, dtype)


def dma(*dims):
    return pltpu.SemaphoreType.DMA(dims)


def per_device(
    node_latent,
    edge_latent,
    send_rows,
    edge_src,
    edge_dst,
    edge_live,
    w_in_blocks,
    w_in_scale,
    bias_in,
    w_out_blocks,
    w_out_scale,
    bias_out,
    norm_gain,
    grad_edge,
    grad_agg,
):
    total, edge_in, node_in, summed = pl.pallas_call(
        main_kernel,
        out_shape=(
            shape((12, 512, 256), BF16),
            shape((512, 512), BF16),
            shape((256, 256), BF16),
            shape((16, 256), F32),
        ),
        in_specs=[
            anywhere(),
            anywhere(),
            vmem(),
            vmem(),
            vmem(),
            smem(),
            anywhere(),
            smem(),
            vmem(),
            anywhere(),
            smem(),
            vmem(),
            vmem(),
            anywhere(),
            anywhere(),
        ],
        out_specs=(anywhere(), vmem(), vmem(), vmem()),
        scratch_shapes=[
            pltpu.VMEM((256, 512), BF16),
            pltpu.VMEM((1536, 768), BF16),
            pltpu.VMEM((768, 512), BF16),
            pltpu.VMEM((256, 512), BF16),
            pltpu.VMEM((512, 512), BF16),
            pltpu.VMEM((2, 12, 512, 256), BF16),
            pltpu.VMEM((2, 8, 256), F32),
            pltpu.VMEM((2, 64, 512), BF16),
            pltpu.VMEM((2, 64, 512), BF16),
            pltpu.VMEM((4, 16, 256), BF16),
            pltpu.VMEM((3, 512, 512), BF16),
            pltpu.VMEM((3, 512, 512), BF16),
            pltpu.VMEM((384, 512), BF16),
            pltpu.VMEM((384, 512), BF16),
            pltpu.VMEM((256, 512), BF16),
            pltpu.VMEM((6, 512, 256), BF16),
            pltpu.VMEM((6, 512, 256), F32),
            pltpu.VMEM((512, 512), F32),
            pltpu.VMEM((512, 512), F32),
            pltpu.VMEM((512, 512), BF16),
            pltpu.VMEM((6, 512, 256), BF16),
            pltpu.VMEM((12, 1024, 256), BF16),
            pltpu.VMEM((6, 1024, 256), BF16),
            pltpu.VMEM((6, 3, 256, 256), BF16),
            pltpu.VMEM((6, 256, 256), BF16),
            pltpu.VMEM((6, 3, 64, 256), BF16),
            pltpu.VMEM((6, 64, 256), BF16),
            pltpu.VMEM((6, 3, 16, 256), BF16),
            pltpu.VMEM((12, 512, 256), BF16),
            pltpu.VMEM((16, 256), F32),
            pltpu.VMEM((1, 16, 256), F32),
            pltpu.VMEM((3, 4, 16, 256), F32),
            pltpu.VMEM((256, 512), F32),
            pltpu.VMEM((128, 512), BF16),
            pltpu.VMEM((2, 64, 512), BF16),
            pltpu.VMEM((256, 256), BF16),
            pltpu.VMEM((256, 256), BF16),
            dma(6),
            dma(6, 8),
            dma(6, 8),
            dma(7),
            dma(7),
            dma(2),
            dma(2),
            dma(6, 10),
            dma(6, 10),
            dma(6, 8),
            dma(6, 8),
            dma(4, 4),
            dma(4, 4),
            dma(3),
            dma(3),
            dma(6),
        ],
        compiler_params=pltpu.CompilerParams(
            collective_id=0, has_side_effects=True, vmem_limit_bytes=LIMIT
        ),
        name="message_grads",
    )(
        node_latent,
        edge_latent,
        send_rows[0],
        edge_src.reshape(8, 128),
        edge_dst.reshape(8, 128),
        edge_live,
        w_in_blocks,
        w_in_scale.T,
        bias_in.reshape(6, 128),
        w_out_blocks,
        w_out_scale.T,
        bias_out.reshape(1, 512),
        norm_gain.reshape(1, 512),
        grad_edge,
        grad_agg,
    )
    grad_w_out, grad_w_in, grad_bias, vectors, grad_edge_in, grad_node = pl.pallas_call(
        finish_kernel,
        out_shape=(
            shape((768, 512), F32),
            shape((1536, 768), F32),
            shape((6, 128), F32),
            shape((3, 512), F32),
            shape((512, 512), BF16),
            shape((256, 256), BF16),
        ),
        in_specs=[anywhere(), anywhere(), anywhere(), vmem()],
        out_specs=(anywhere(), anywhere(), vmem(), vmem(), anywhere(), anywhere()),
        scratch_shapes=[
            pltpu.VMEM((12, 512, 256), BF16),
            pltpu.VMEM((12, 512, 256), F32),
            dma(14),
            dma(13),
        ],
        compiler_params=pltpu.CompilerParams(vmem_limit_bytes=LIMIT),
        name="widen_grads",
    )(total, edge_in, node_in, summed)
    return (grad_edge_in, grad_node, grad_w_in, grad_bias.reshape(768), grad_w_out, vectors)


def solution(mesh):
    in_specs = (
        P("dom", None),
        P("dom", None),
        P("dom", None, None),
        P("dom"),
        P("dom"),
        P("dom"),
        P(None, "hid"),
        P(None, "hid"),
        P("hid"),
        P("hid", None),
        P("hid", None),
        P(),
        P(),
        P("dom", None),
        P("dom", None),
    )
    out_specs = (
        P(("dom", "hid"), None),
        P("dom", "hid"),
        P(None, "hid"),
        P("hid"),
        P("hid", None),
        P(),
    )
    return jax.shard_map(
        per_device, mesh=mesh, in_specs=in_specs, out_specs=out_specs, check_vma=False
    )
```

time: 827 us -> 107 us (0.13)
  waiting for transfers between devices: 449 us -> 0 us
  blocking collectives: 273 us -> 0 us
  Pallas kernels: 0 us -> 105 us
  local copies, waits for them, and re-layouts: 32.9 us -> 0 us
  matrix products: 25.9 us -> 0 us
  other arithmetic: 17.8 us -> 0 us
  between operations: 14.9 us -> 1.45 us
  starting transfers between devices: 12.4 us -> 0 us
    psum x2 -> x0, waiting for transfers between devices: 358 us -> none  [the longest x1 287 us: per_device(): lax.psum((grad_w_first, grad_bias_local, grad_w_second, vectors), 'dom')]
    psum x1 -> x0, blocking collectives: 273 us -> none  [per_device(): lax.psum((grad_w_first, grad_bias_local, grad_w_second, vectors), 'dom')]
    pallas_call x0 -> x2, Pallas kernels: none -> 105 us  [the longest x1 82.8 us: per_device(): pl.pallas_call(main_kernel, out_shape=(shape((12, 512, 256), BF16), shape...]
    reduce_scatter x2 -> x0, waiting for transfers between devices: 91.6 us -> none  [the longest x1 79.9 us: per_device(): lax.psum_scatter(contract_cols(grad_pre_low, w_first), 'hid', scatter_dim...]
    dot_general x7 -> x0, matrix products: 25.9 us -> none  [the longest x2 8.46 us: contract_rows(): lax.dot_general(left_side, right_side, (((0,), (0,)), ((), ())), preferre...]
    unnamed x64 -> x0, local copies, waits for them, and re-layouts: 15.5 us -> none
    gather x5 -> x0, local copies, waits for them, and re-layouts: 15.3 us -> none  [the longest x1 3.97 us: per_device(): jnp.take(grad_agg, edge_dst, axis=0).astype(jnp.float32)]
    ppermute x4 -> x0, starting transfers between devices: 12.1 us -> none  [passed_along(): return lax.ppermute(block, axis, route)]
  transfers between devices with their start and end apart: 8 -> 0, of which waited for: 4 -> 0; matrix products, arithmetic and copies ran while one was open for 4% -> 0% of each run, Pallas kernels for 0% -> 0%
where the time goes in v2:
time: 107 us
  Pallas kernels  105 us (98%)
  between operations  1.45 us (1%)
    pallas_call x1, Pallas kernels, per_device(): pl.pallas_call(main_kernel, out_shape=(shape((12, 512, 256), BF16), shape...  82.8 us
    pallas_call x1, Pallas kernels, per_device(): pl.pallas_call(finish_kernel, out_shape=(shape((768, 512), F32), shape((1...  22.5 us

profile of v2, /device:TPU:1, one launch (start us, length us, event | category | flops | bytes accessed | tf_op | source)
XLA Modules:
  0.0 106.8 jit_solution(13599246730773197757)
XLA Ops:
  1.3 82.8 %message_grads.1 = (bf16[12,512,256]{2,1,0:T(8,128)(2,1)}, bf16[512,512]{1,0:T(8,128)(2,1)}, bf16[256,256]{1,0:T(8,128)(2,1)}, f32[16,256]{1,0:T(8,128)}) custom-call(bf16[256,512]{1,0:T(8,128)(2,1)} %node_hbm.1, bf16[1024,512]{1,0:T(8,128)(2,1)} %edge_hbm.1, s32[2,64]{1,0:T(2,128)} %bitcast.16, s32[8,128]{1,0:T(8,128)} %bitcast.9, s32[8,128]{1,0:T(8,128)} %bitcast.10, ...), custom_call_target="tpu_custom_call" | custom-call | tf_op jit(solution)/shard_map/message_grads/pallas_call | solution.py:775
  84.1 22.5 %widen_grads.1 = (f32[768,512]{1,0:T(8,128)}, f32[1536,768]{1,0:T(8,128)}, f32[6,128]{1,0:T(8,128)}, f32[3,512]{1,0:T(4,128)}, bf16[512,512]{1,0:T(8,128)(2,1)}, /*index=5*/bf16[256,256]{1,0:T(8,128)(2,1)}) custom-call(bf16[12,512,256]{2,1,0:T(8,128)(2,1)} %get-tuple-element.16.total, bf16[512,512]{1,0:T(8,128)(2,1)} %get-tuple-element.17.edge_in, ...), custom_call_target="tpu_custom_call" | custom-call | tf_op jit(solution)/shard_map/widen_grads/pallas_call | solution.py:877

commit v3 on v2

--- a/solution.py
+++ b/solution.py
@@ -65,17 +65,26 @@
     )
 
 
-def kind(chunk):
-    return chunk % 3
-
-
-def own_tile(place, chunk, yl=None):
+AXES = (
+    ("z", "x", "y"),
+    ("x", "z", "y"),
+    ("y", "z", "x"),
+    ("z", "x", "y"),
+    ("x", "z", "y"),
+    ("y", "x", "z"),
+)
+
+
+def tiles_known(chunk):
+    return 2 if AXES[chunk][2] == "y" else 4
+
+
+def first_tile(place, chunk, yl=None):
     yl = place.yl if yl is None else yl
-    if kind(chunk) == 0:
-        return (place.z * 4 + place.x) * 2 + yl
-    if kind(chunk) == 1:
-        return (place.x * 2 + yl) * 4 + place.z
-    return (yl * 4 + place.z) * 4 + place.x
+    a, b, _ = AXES[chunk]
+    if a == "y":
+        return (yl * 4 + getattr(place, b)) * 4
+    return (getattr(place, a) * 4 + getattr(place, b)) * 2
 
 
 def rows_of(first, count, unit=16):
@@ -83,27 +92,14 @@
 
 
 def gather_steps(place, chunk):
-    z, x, yl = place.z, place.x, place.yl
-    z_ring = [place.ring("z", j) for j in (1, 2, 3)]
-    x_ring = [place.ring("x", j) for j in (1, 2, 3)]
-    pair = [place.pair()]
-    if kind(chunk) == 0:
-        return [
-            ((z * 4 + x) * 2 + yl, 1, pair),
-            ((z * 4 + x) * 2, 2, x_ring),
-            (z * 8, 8, z_ring),
-        ]
-    if kind(chunk) == 1:
-        return [
-            ((x * 2 + yl) * 4 + z, 1, z_ring),
-            ((x * 2 + yl) * 4, 4, pair),
-            (x * 8, 8, x_ring),
-        ]
-    return [
-        ((yl * 4 + z) * 4 + x, 1, x_ring),
-        ((yl * 4 + z) * 4, 4, z_ring),
-        (yl * 16, 16, pair),
-    ]
+    a, b, _ = AXES[chunk]
+    ring = [place.ring(b, j) for j in (1, 2, 3)]
+    known = tiles_known(chunk)
+    if a == "y":
+        last = (place.yl * 16, 16, [place.pair()])
+    else:
+        last = (getattr(place, a) * 8, 8, [place.ring(a, j) for j in (1, 2, 3)])
+    return [(first_tile(place, chunk), known, ring), last]
 
 
 class Gather:
@@ -118,14 +114,14 @@
         if chunk not in self.steps:
             self.steps[chunk] = gather_steps(place, chunk)
         block = 2 * chunk + place.core
-        if step == 3:
+        if step == 2:
             first, count, targets = 0, 32, [place.other_core()]
-            base = 7
+            base = 6
         else:
             first, count, targets = self.steps[chunk][step]
             base = sum(len(s[2]) for s in self.steps[chunk][:step])
         part = self.buf.at[block, rows_of(first, count)]
-        goal = self.result.at[block] if step == 3 else part
+        goal = self.result.at[block] if step == 2 else part
         copies = []
         for j, target in enumerate(targets):
             copy = remote(
@@ -146,7 +142,8 @@
 
 
 RING = (1, 2, 3)
-REDUCE_AXES = {0: ("z", "x", "y"), 1: ("x", "y", "z"), 2: ("y", "z", "x")}
+GATHERED = (3, 4, 2, 1, 5)
+DIRECT = (0,)
 
 
 def tdot(a, b):
@@ -189,19 +186,31 @@
     lax.fori_loop(first, last, block, 0)
 
 
-def dequantize_tile(tile, w_in_ref, scales, index, q):
+def dequantize_tiles(tile, w_in_ref, scales, index, q, count):
     j = lax.div(index, 3)
     r = lax.rem(index, 3)
-    rows = pl.ds(pl.multiple_of(512 * r + 16 * q, 16), 16)
+    rows = pl.ds(pl.multiple_of(512 * r + 16 * q, 16), 16 * count)
     for b in range(2):
         scale = scales[2 * j + b, 4 * r + lax.div(q, 8)]
         cols = pl.ds(pl.multiple_of(256 * j + 128 * b, 128), 128)
-        tile[:, 128 * b : 128 * b + 128] = (w_in_ref[rows, cols].astype(F32) * scale).astype(BF16)
+        tile[0 : 16 * count, 128 * b : 128 * b + 128] = (w_in_ref[rows, cols].astype(F32) * scale).astype(BF16)
+
+
+def dequantize_out_tiles(tile, w_out_ref, scales, q, wanted):
+    side = lax.div(q, 16)
+    row = lax.rem(q, 16)
+    rows = pl.ds(pl.multiple_of(512 + 16 * row, 16), 32)
+    for b in range(2):
+        scale = scales[2 * side + b, 4 + lax.div(row, 8)]
+        cols = pl.ds(pl.multiple_of(256 * side + 128 * b, 128), 128)
+        value = w_out_ref[rows, cols].astype(F32) * scale
+        kept = tile[0:32, 128 * b : 128 * b + 128].astype(F32)
+        tile[0:32, 128 * b : 128 * b + 128] = jnp.where(wanted, value, kept).astype(BF16)
 
 
 def place_rows(grads, block, first, value, half):
     count = value.shape[0]
-    group = {0: 32, 1: 128, 2: 512}[kind(block // 2)]
+    group = 512 if AXES[block // 2][0] == "y" else 32
     size = min(group, count)
     for at in range(0, count, size):
         row = first + at
@@ -237,7 +246,7 @@
         self.send(chunk, 0, 0, src, self.core_in.at[chunk], self.place.other_core())
 
     def spread(self, chunk, level, src, dst, unit):
-        axis = REDUCE_AXES[kind(chunk)][level]
+        axis = AXES[chunk][level]
         mine = getattr(self.place, axis)
         for j in RING:
             at = lax.rem(mine + j, 4)
@@ -245,7 +254,7 @@
             self.send(chunk, level + 1, 3 * level + j, part, dst.at[j - 1], self.place.ring(axis, j))
 
     def kept(self, chunk, level, src, unit):
-        mine = getattr(self.place, REDUCE_AXES[kind(chunk)][level])
+        mine = getattr(self.place, AXES[chunk][level])
         return src[rows_of(mine, 1, unit), :].astype(F32)
 
     def add_core(self, chunk):
@@ -275,13 +284,28 @@
         for j in range(3):
             value = value + self.second_in[chunk, j].astype(F32)
         self.second_out[chunk] = value.astype(BF16)
-        self.spread(chunk, 2, self.second_out.at[chunk], self.third_in.at[chunk], 16)
+        axis = AXES[chunk][2]
+        mine = getattr(self.place, axis)
+        rows = 16 * tiles_known(chunk)
+        if axis == "y":
+            self.third_in[chunk, mine, 0:rows, :] = self.second_out[chunk, rows_of(self.place.hid, 1, 32), :]
+        else:
+            self.third_in[chunk, mine] = self.second_out[chunk]
+        for j in RING:
+            if axis == "y":
+                half = lax.div(lax.rem(mine + j, 4), 2)
+                part = self.second_out.at[chunk, rows_of(half, 1, 32)]
+            else:
+                part = self.second_out.at[chunk]
+            goal = self.third_in.at[chunk, mine, pl.ds(0, rows)]
+            self.send(chunk, 3, 6 + j, part, goal, self.place.ring(axis, j))
 
     def add_third(self, chunk):
         self.arrived(chunk, 3)
-        value = self.kept(chunk, 2, self.second_out.at[chunk], 16)
-        for j in range(3):
-            value = value + self.third_in[chunk, j].astype(F32)
+        rows = 16 * tiles_known(chunk)
+        value = self.third_in[chunk, 0, 0:rows, :].astype(F32)
+        for at in range(1, 4):
+            value = value + self.third_in[chunk, at, 0:rows, :].astype(F32)
         return value
 
 
@@ -390,57 +414,62 @@
     for j in range(3):
         bias[0, j : j + 1, 0:128] = bias_ref[2 * j : 2 * j + 1, :]
         bias[0, j : j + 1, 128:256] = bias_ref[2 * j + 1 : 2 * j + 2, :]
-    get_w_in.wait()
-    tile_at = {}
-    for chunk in (2, 3, 4, 5):
-        tile_at[chunk] = own_tile(place, chunk, 1 - place.yl)
-        dequantize_tile(tiles.at[chunk - 2], w_in, w_in_scale, 2 * chunk + core - 3, tile_at[chunk])
-    dequantize_in(own, w_in, w_in_scale, 0, 1)
-    get_w_out.wait()
-    dequantize_out(own, w_out, w_out_scale)
-    all_here()
-    crossing = {}
-    for chunk in (2, 3, 4, 5, 1, 0):
-        block = 2 * chunk + core
-        if chunk < 2:
-            src, dst = own.at[block], other.at[block]
-        else:
-            src, dst = tiles.at[chunk - 2], other.at[block, rows_of(tile_at[chunk], 1)]
-        crossing[chunk] = go(src, dst, cross_send.at[chunk], cross_recv.at[chunk], place.cross())
-    bias_copy = go(bias.at[0], bias.at[1], cross_send.at[6], cross_recv.at[6], place.cross())
-    get_node.wait()
-    for side in (0, 1):
-        picks = (lax.broadcasted_iota(jnp.int32, (256, 64), 0) == send_ref[side : side + 1, :]).astype(F32)
-        halo_out[side] = tdot(picks.astype(BF16), node[...]).astype(BF16)
-    up_rows = go(halo_out.at[1], halo.at[0], halo_send.at[0], halo_recv.at[0], place.partition(1))
-    down_rows = go(halo_out.at[0], halo.at[1], halo_send.at[1], halo_recv.at[1], place.partition(63))
     for k in range(4):
         cols = slice(128 * k, 128 * k + 128)
         src_row = src_ref[pl.ds(4 * hid + k, 1), :]
         dst_row = dst_ref[pl.ds(4 * hid + k, 1), :]
         pick_src[:, cols] = (lax.broadcasted_iota(jnp.int32, (384, 128), 0) == src_row).astype(F32).astype(BF16)
         pick_dst[:, cols] = (lax.broadcasted_iota(jnp.int32, (256, 128), 0) == dst_row).astype(F32).astype(BF16)
+    get_node.wait()
+    for side in (0, 1):
+        picks = (lax.broadcasted_iota(jnp.int32, (256, 64), 0) == send_ref[side : side + 1, :]).astype(F32)
+        halo_out[side] = tdot(picks.astype(BF16), node[...]).astype(BF16)
+    get_w_in.wait()
+    tile_at = {}
+    for chunk in GATHERED:
+        known = tiles_known(chunk)
+        index = 2 * chunk + core - 3
+        if chunk == 1:
+            index = 0
+        tile_at[chunk] = first_tile(place, chunk, 1 - place.yl)
+        dequantize_tiles(tiles.at[chunk - 1], w_in, w_in_scale, index, tile_at[chunk], known)
+    get_w_out.wait()
+    dequantize_out_tiles(tiles.at[0], w_out, w_out_scale, tile_at[1], core == 0)
+    all_here()
+    crossing = {}
+
+    def cross(chunk, src, dst):
+        crossing[chunk] = go(src, dst, cross_send.at[chunk], cross_recv.at[chunk], place.cross())
+
+    for chunk in GATHERED:
+        rows = 16 * tiles_known(chunk)
+        goal = other.at[2 * chunk + core, pl.ds(pl.multiple_of(16 * tile_at[chunk], 16), rows)]
+        cross(chunk, tiles.at[chunk - 1, pl.ds(0, rows)], goal)
+    up_rows = go(halo_out.at[1], halo.at[0], halo_send.at[0], halo_recv.at[0], place.partition(1))
+    down_rows = go(halo_out.at[0], halo.at[1], halo_send.at[1], halo_recv.at[1], place.partition(63))
+    bias_copy = go(bias.at[0], bias.at[1], cross_send.at[6], cross_recv.at[6], place.cross())
+    dequantize_out(own, w_out, w_out_scale)
+    dequantize_in(own, w_in, w_in_scale, 0, 1)
+    for chunk in DIRECT:
+        cross(chunk, own.at[2 * chunk + core], other.at[2 * chunk + core])
     spread = Gather(place, other, spread_send, spread_recv, other)
-    for chunk in (2, 3, 4, 5):
+    for chunk in GATHERED:
         crossing[chunk].wait_recv()
         spread.start(chunk, 0)
     dequantize_in(own, w_in, w_in_scale, 1, 9)
-    for chunk in (2, 3, 4, 5):
-        spread.arrived(chunk, 0)
-        spread.start(chunk, 1)
     inp[2] = tdot(pick_dst[...], node[...]).astype(BF16)
     get_agg.wait()
     up[...] = tdot(pick_dst[...], gagg[...])
     ext[0:256] = node[...]
+    for chunk in GATHERED:
+        spread.arrived(chunk, 0)
+        spread.start(chunk, 1)
     up_rows.wait_recv()
     down_rows.wait_recv()
     ext[256:320] = jnp.where(dom > 0, halo[0], jnp.zeros((64, 512), BF16))
     ext[320:384] = jnp.where(dom < 63, halo[1], jnp.zeros((64, 512), BF16))
     inp[1] = tdot(pick_src[...], ext[...]).astype(BF16)
     get_edge.wait()
-    for chunk in (2, 3, 4, 5):
-        spread.arrived(chunk, 1)
-        spread.start(chunk, 2)
 
     def forward(slot, j):
         pre = bias[slot, pl.ds(j, 1), :]
@@ -456,26 +485,25 @@
         return 0
 
     lax.fori_loop(0, 3, forward_own, 0)
-    crossing[1].wait_recv()
-    spread.start(1, 3)
-    for chunk in (2, 3, 4, 5):
-        spread.arrived(chunk, 2)
-        spread.start(chunk, 3)
-    crossing[0].wait_recv()
-    spread.start(0, 3)
+    for chunk in DIRECT:
+        crossing[chunk].wait_recv()
+        spread.start(chunk, 2)
+    for chunk in GATHERED:
+        spread.arrived(chunk, 1)
+        spread.start(chunk, 2)
     for r in range(3):
         inpt[r] = inp[r].T
     get_cot.wait()
     bias_copy.wait_recv()
+    for chunk in (3, 4):
+        spread.arrived(chunk, 2)
+    forward(1, 1)
     for chunk in (1, 2):
-        spread.arrived(chunk, 3)
+        spread.arrived(chunk, 2)
     forward(1, 0)
-    for chunk in (3, 4):
-        spread.arrived(chunk, 3)
-    forward(1, 1)
-    spread.arrived(5, 3)
+    spread.arrived(5, 2)
     forward(1, 2)
-    spread.arrived(0, 3)
+    spread.arrived(0, 2)
 
     for side in range(2):
         result = bias_out_ref[:, 256 * side : 256 * side + 256]
@@ -637,17 +665,15 @@
             reduce.add_second(chunk)
         elif name == "third":
             value = reduce.add_third(chunk) * (1.0 / 1024)
-            total[2 * chunk + core, rows_of(own_tile(place, chunk), 1), :] = value.astype(BF16)
+            rows = pl.ds(pl.multiple_of(16 * first_tile(place, chunk), 16), 16 * tiles_known(chunk))
+            total[2 * chunk + core, rows, :] = value.astype(BF16)
             gather.start(chunk, 0)
         elif name == "gather":
             gather.arrived(chunk, 0)
             gather.start(chunk, 1)
-        elif name == "more":
+        else:
             gather.arrived(chunk, 1)
             gather.start(chunk, 2)
-        else:
-            gather.arrived(chunk, 2)
-            gather.start(chunk, 3)
             write(chunk)
 
     produce(1)
@@ -660,13 +686,10 @@
     stage("add", 3)
     produce(5)
     events = []
-    for name, chunk_at in (("add", 2.0), ("first", 9.0), ("second", 13.5), ("third", 17.5)):
+    for name, chunk_at in (("add", 2.0), ("first", 9.0), ("second", 13.5), ("third", 17.5), ("gather", 21.5), ("last", 27.5)):
         for chunk in range(CHUNKS):
             if name != "add" or chunk > 3:
                 events.append((chunk_at + 2.0 * chunk, name, chunk))
-    for name, chunk_at in (("gather", 21.5), ("more", 25.5), ("last", 31.5)):
-        for chunk in range(CHUNKS):
-            events.append((chunk_at + 2.0 * chunk, name, chunk))
     for extra_at, run in ((8.5, extra_a), (10.2, extra_b), (11.2, extra_c), (14.4, extra_d), (19.0, extra_e), (25.0, extra_f)):
         events.append((extra_at, "run", run))
     for _, name, item in sorted(events, key=lambda event: event[0]):
@@ -675,7 +698,7 @@
         else:
             stage(name, item)
     for chunk in range(CHUNKS):
-        gather.arrived(chunk, 3)
+        gather.arrived(chunk, 2)
     spread.sent()
     reduce.sent()
     gather.sent()
@@ -694,12 +717,8 @@
     ]
     for copy in moves:
         copy.start()
-    through = [
-        pltpu.make_async_copy(edge_in, grad_edge, read_sem.at[12]),
-        pltpu.make_async_copy(node_in, grad_node, read_sem.at[13]),
-    ]
-    for copy in through:
-        copy.start()
+    grad_edge[...] = edge_in[...]
+    grad_node[...] = node_in[...]
     for i in range(3):
         vectors[i : i + 1, 0:256] = summed[6 + 2 * i : 7 + 2 * i, :]
         vectors[i : i + 1, 256:512] = summed[7 + 2 * i : 8 + 2 * i, :]
@@ -731,7 +750,7 @@
             copy = pltpu.make_async_copy(src, dst, write_sem.at[len(writes)])
             copy.start()
             writes.append(copy)
-    for copy in writes + through:
+    for copy in writes:
         copy.wait()
 
 
@@ -808,7 +827,7 @@
             pltpu.VMEM((2, 8, 256), F32),
             pltpu.VMEM((2, 64, 512), BF16),
             pltpu.VMEM((2, 64, 512), BF16),
-            pltpu.VMEM((4, 16, 256), BF16),
+            pltpu.VMEM((5, 64, 256), BF16),
             pltpu.VMEM((3, 512, 512), BF16),
             pltpu.VMEM((3, 512, 512), BF16),
             pltpu.VMEM((384, 512), BF16),
@@ -826,7 +845,7 @@
             pltpu.VMEM((6, 256, 256), BF16),
             pltpu.VMEM((6, 3, 64, 256), BF16),
             pltpu.VMEM((6, 64, 256), BF16),
-            pltpu.VMEM((6, 3, 16, 256), BF16),
+            pltpu.VMEM((6, 4, 64, 256), BF16),
             pltpu.VMEM((12, 512, 256), BF16),
             pltpu.VMEM((16, 256), F32),
             pltpu.VMEM((1, 16, 256), F32),
@@ -884,12 +903,12 @@
             shape((512, 512), BF16),
             shape((256, 256), BF16),
         ),
-        in_specs=[anywhere(), anywhere(), anywhere(), vmem()],
-        out_specs=(anywhere(), anywhere(), vmem(), vmem(), anywhere(), anywhere()),
+        in_specs=[anywhere(), vmem(), vmem(), vmem()],
+        out_specs=(anywhere(), anywhere(), vmem(), vmem(), vmem(), vmem()),
         scratch_shapes=[
             pltpu.VMEM((12, 512, 256), BF16),
             pltpu.VMEM((12, 512, 256), F32),
-            dma(14),
+            dma(12),
             dma(13),
         ],
         compiler_params=pltpu.CompilerParams(vmem_limit_bytes=LIMIT),

time: 107 us -> 88.2 us (0.82)
  Pallas kernels: 105 us -> 85.7 us
    pallas_call x1, Pallas kernels: 22.5 us -> 5.81 us  [per_device(): pl.pallas_call(finish_kernel, out_shape=(shape((768, 512), F32), shape((1...]
    pallas_call x1, Pallas kernels: 82.8 us -> 79.9 us  [per_device(): pl.pallas_call(main_kernel, out_shape=(shape((12, 512, 256), BF16), shape...]
where the time goes in v3:
time: 88.2 us; the launch traced here: 87.1 us
  Pallas kernels  85.7 us (97%)
  between operations  1.45 us (2%)
    pallas_call x1, Pallas kernels, per_device(): pl.pallas_call(main_kernel, out_shape=(shape((12, 512, 256), BF16), shape...  79.9 us
    pallas_call x1, Pallas kernels, per_device(): pl.pallas_call(finish_kernel, out_shape=(shape((768, 512), F32), shape((1...  5.81 us

profile of v3, /device:TPU:1, one launch (start us, length us, event | category | flops | bytes accessed | tf_op | source)
XLA Modules:
  0.0 87.1 jit_solution(15550860180543268775)
XLA Ops:
  1.3 79.9 %message_grads.1 = (bf16[12,512,256]{2,1,0:T(8,128)(2,1)}, bf16[512,512]{1,0:T(8,128)(2,1)}, bf16[256,256]{1,0:T(8,128)(2,1)}, f32[16,256]{1,0:T(8,128)}) custom-call(bf16[256,512]{1,0:T(8,128)(2,1)} %node_hbm.1, bf16[1024,512]{1,0:T(8,128)(2,1)} %edge_hbm.1, s32[2,64]{1,0:T(2,128)} %bitcast.16, s32[8,128]{1,0:T(8,128)} %bitcast.9, s32[8,128]{1,0:T(8,128)} %bitcast.10, ...), custom_call_target="tpu_custom_call" | custom-call | tf_op jit(solution)/shard_map/message_grads/pallas_call | solution.py:794
  81.2 5.8 %widen_grads.1 = (f32[768,512]{1,0:T(8,128)}, f32[1536,768]{1,0:T(8,128)}, f32[6,128]{1,0:T(8,128)}, f32[3,512]{1,0:T(4,128)}, bf16[512,512]{1,0:T(8,128)(2,1)}, /*index=5*/bf16[256,256]{1,0:T(8,128)(2,1)}) custom-call(bf16[12,512,256]{2,1,0:T(8,128)(2,1)} %get-tuple-element.16.total, bf16[512,512]{1,0:T(8,128)(2,1)} %get-tuple-element.17.edge_in, ...), custom_call_target="tpu_custom_call" | custom-call | tf_op jit(solution)/shard_map/widen_grads/pallas_call | solution.py:896

commit v4 on v3

--- a/solution.py
+++ b/solution.py
@@ -218,6 +218,14 @@
         grads[block, pl.ds(pl.multiple_of(base + group * half, 32), size), :] = value[at : at + size]
 
 
+ORDER = (
+    "P1", "A0", "P2", "A1", "P3", "A2", "P4", "A3", "P5", "A4", "A5", "F0",
+    "Xa", "F1", "F2", "F3", "Xb", "S0", "F4", "S1", "F5", "S2", "S3", "Xd",
+    "T0", "S4", "T1", "S5", "T2", "Xe", "T3", "T4", "T5", "G0", "G1", "G2",
+    "G3", "Xc", "G4", "G5", "Xf", "L0", "L1", "L2", "L3", "L4", "L5",
+)
+
+
 class Reduce:
     def __init__(self, place, grads, core_in, first_in, first_out, second_in, second_out, third_in, send_sem, recv_sem):
         self.place, self.grads, self.core_in = place, grads, core_in
@@ -263,8 +271,7 @@
 
         def part(i, _):
             rows = pl.ds(pl.multiple_of(i * 128, 128), 128)
-            mine = self.grads[block, rows, :].astype(F32)
-            self.grads[block, rows, :] = (mine + self.core_in[chunk, rows, :].astype(F32)).astype(BF16)
+            self.grads[block, rows, :] = self.grads[block, rows, :] + self.core_in[chunk, rows, :]
             return 0
 
         lax.fori_loop(0, 8, part, 0)
@@ -657,18 +664,18 @@
         writes.append(copy)
 
     def stage(name, chunk):
-        if name == "add":
+        if name == "A":
             reduce.add_core(chunk)
-        elif name == "first":
+        elif name == "F":
             reduce.add_first(chunk)
-        elif name == "second":
+        elif name == "S":
             reduce.add_second(chunk)
-        elif name == "third":
+        elif name == "T":
             value = reduce.add_third(chunk) * (1.0 / 1024)
             rows = pl.ds(pl.multiple_of(16 * first_tile(place, chunk), 16), 16 * tiles_known(chunk))
             total[2 * chunk + core, rows, :] = value.astype(BF16)
             gather.start(chunk, 0)
-        elif name == "gather":
+        elif name == "G":
             gather.arrived(chunk, 0)
             gather.start(chunk, 1)
         else:
@@ -676,27 +683,14 @@
             gather.start(chunk, 2)
             write(chunk)
 
-    produce(1)
-    stage("add", 0)
-    produce(2)
-    stage("add", 1)
-    produce(3)
-    stage("add", 2)
-    produce(4)
-    stage("add", 3)
-    produce(5)
-    events = []
-    for name, chunk_at in (("add", 2.0), ("first", 9.0), ("second", 13.5), ("third", 17.5), ("gather", 21.5), ("last", 27.5)):
-        for chunk in range(CHUNKS):
-            if name != "add" or chunk > 3:
-                events.append((chunk_at + 2.0 * chunk, name, chunk))
-    for extra_at, run in ((8.5, extra_a), (10.2, extra_b), (11.2, extra_c), (14.4, extra_d), (19.0, extra_e), (25.0, extra_f)):
-        events.append((extra_at, "run", run))
-    for _, name, item in sorted(events, key=lambda event: event[0]):
-        if name == "run":
-            item()
+    work = {"a": extra_a, "b": extra_b, "c": extra_c, "d": extra_d, "e": extra_e, "f": extra_f}
+    for name, item in ORDER:
+        if name == "X":
+            work[item]()
+        elif name == "P":
+            produce(int(item))
         else:
-            stage(name, item)
+            stage(name, int(item))
     for chunk in range(CHUNKS):
         gather.arrived(chunk, 2)
     spread.sent()

time: 88.2 us -> 82.6 us (0.937)
  Pallas kernels: 85.7 us -> 80.9 us
    pallas_call x1, Pallas kernels: 79.9 us -> 75.1 us  [per_device(): pl.pallas_call(main_kernel, out_shape=(shape((12, 512, 256), BF16), shape...]
where the time goes in v4:
time: 82.6 us; the launch traced here: 82.4 us
  Pallas kernels  80.9 us (98%)
  between operations  1.45 us (2%)
    pallas_call x1, Pallas kernels, per_device(): pl.pallas_call(main_kernel, out_shape=(shape((12, 512, 256), BF16), shape...  75.1 us
    pallas_call x1, Pallas kernels, per_device(): pl.pallas_call(finish_kernel, out_shape=(shape((768, 512), F32), shape((1...  5.81 us

profile of v4, /device:TPU:1, one launch (start us, length us, event | category | flops | bytes accessed | tf_op | source)
XLA Modules:
  0.0 82.4 jit_solution(7752641128915230651)
XLA Ops:
  1.3 75.1 %message_grads.1 = (bf16[12,512,256]{2,1,0:T(8,128)(2,1)}, bf16[512,512]{1,0:T(8,128)(2,1)}, bf16[256,256]{1,0:T(8,128)(2,1)}, f32[16,256]{1,0:T(8,128)}) custom-call(bf16[256,512]{1,0:T(8,128)(2,1)} %node_hbm.1, bf16[1024,512]{1,0:T(8,128)(2,1)} %edge_hbm.1, s32[2,64]{1,0:T(2,128)} %bitcast.16, s32[8,128]{1,0:T(8,128)} %bitcast.9, s32[8,128]{1,0:T(8,128)} %bitcast.10, ...), custom_call_target="tpu_custom_call" | custom-call | tf_op jit(solution)/shard_map/message_grads/pallas_call | solution.py:788
  76.4 5.8 %widen_grads.1 = (f32[768,512]{1,0:T(8,128)}, f32[1536,768]{1,0:T(8,128)}, f32[6,128]{1,0:T(8,128)}, f32[3,512]{1,0:T(4,128)}, bf16[512,512]{1,0:T(8,128)(2,1)}, /*index=5*/bf16[256,256]{1,0:T(8,128)(2,1)}) custom-call(bf16[12,512,256]{2,1,0:T(8,128)(2,1)} %get-tuple-element.16.total, bf16[512,512]{1,0:T(8,128)(2,1)} %get-tuple-element.17.edge_in, ...), custom_call_target="tpu_custom_call" | custom-call | tf_op jit(solution)/shard_map/widen_grads/pallas_call | solution.py:890

commit v5 on v4

--- a/solution.py
+++ b/solution.py
@@ -93,12 +93,12 @@
 
 def gather_steps(place, chunk):
     a, b, _ = AXES[chunk]
-    ring = [place.ring(b, j) for j in (1, 2, 3)]
+    ring = [place.ring(b, j) for j in (2, 1, 3)]
     known = tiles_known(chunk)
     if a == "y":
         last = (place.yl * 16, 16, [place.pair()])
     else:
-        last = (getattr(place, a) * 8, 8, [place.ring(a, j) for j in (1, 2, 3)])
+        last = (getattr(place, a) * 8, 8, [place.ring(a, j) for j in (2, 1, 3)])
     return [(first_tile(place, chunk), known, ring), last]
 
 
@@ -113,23 +113,24 @@
         place = self.place
         if chunk not in self.steps:
             self.steps[chunk] = gather_steps(place, chunk)
-        block = 2 * chunk + place.core
+        halved = AXES[chunk][0] == "y"
         if step == 2:
-            first, count, targets = 0, 32, [place.other_core()]
-            base = 6
-        else:
-            first, count, targets = self.steps[chunk][step]
-            base = sum(len(s[2]) for s in self.steps[chunk][:step])
+            first, count = ((1 - place.yl) * 16, 16) if halved else (0, 32)
+            self.send(chunk, 2, first, count, 6, place.other_core())
+            return
+        first, count, targets = self.steps[chunk][step]
+        for j, target in enumerate(targets):
+            self.send(chunk, step, first, count, 3 * step + j, target)
+        if step == 1 and halved:
+            self.send(chunk, 2, first, count, 7, place.other_core())
+
+    def send(self, chunk, step, first, count, index, target):
+        block = 2 * chunk + self.place.core
         part = self.buf.at[block, rows_of(first, count)]
-        goal = self.result.at[block] if step == 2 else part
-        copies = []
-        for j, target in enumerate(targets):
-            copy = remote(
-                part, goal, self.send_sem.at[chunk, base + j], self.recv_sem.at[chunk, base + j], target
-            )
-            copy.start()
-            copies.append(copy)
-        self.flying[chunk, step] = copies
+        goal = self.result.at[block, rows_of(first, count)] if step == 2 else part
+        copy = remote(part, goal, self.send_sem.at[chunk, index], self.recv_sem.at[chunk, index], target)
+        copy.start()
+        self.flying.setdefault((chunk, step), []).append(copy)
 
     def arrived(self, chunk, step):
         for copy in self.flying[chunk, step]:
@@ -141,7 +142,7 @@
                 copy.wait_send()
 
 
-RING = (1, 2, 3)
+RING = (2, 1, 3)
 GATHERED = (3, 4, 2, 1, 5)
 DIRECT = (0,)
 
@@ -373,6 +374,8 @@
     halo_in,
     node_out,
     node_in,
+    third_vector,
+    act_turned,
     local_sem,
     spread_send,
     spread_recv,
@@ -478,6 +481,33 @@
     inp[1] = tdot(pick_src[...], ext[...]).astype(BF16)
     get_edge.wait()
 
+    live = live_ref[0] - hid * 512
+
+    def fold(value):
+        return jnp.sum(value.reshape(8, 8, 512), axis=0)
+
+    def mask_upstream(i, carry):
+        rows = pl.ds(pl.multiple_of(i * 64, 64), 64)
+        mask = (lax.broadcasted_iota(jnp.int32, (64, 512), 0) + i * 64) < live
+        upstream = jnp.where(mask, gedge[rows, :].astype(F32) + up[rows, :], 0.0)
+        up[rows, :] = upstream
+        return carry + fold(upstream)
+
+    def message_part(slot, side):
+        result = dot(act[3 * slot + 2], weights[slot, 2, 256 * side : 256 * side + 256, :])
+        for j in range(2):
+            result = result + dot(act[3 * slot + j], weights[slot, side, 256 * j : 256 * j + 256, :])
+        return result
+
+    def prepare():
+        for side in range(2):
+            cols = slice(256 * side, 256 * side + 256)
+            msg[:, cols] = bias_out_ref[:, cols] + message_part(0, side)
+        get_cot.wait()
+        third_vector[...] = lax.fori_loop(0, 8, mask_upstream, jnp.zeros((8, 512), F32))
+        for j in range(3):
+            act_turned[j] = act[j].T
+
     def forward(slot, j):
         pre = bias[slot, pl.ds(j, 1), :]
         for r in range(3):
@@ -500,7 +530,7 @@
         spread.start(chunk, 2)
     for r in range(3):
         inpt[r] = inp[r].T
-    get_cot.wait()
+    prepare()
     bias_copy.wait_recv()
     for chunk in (3, 4):
         spread.arrived(chunk, 2)
@@ -513,21 +543,14 @@
     spread.arrived(0, 2)
 
     for side in range(2):
-        result = bias_out_ref[:, 256 * side : 256 * side + 256]
-        for slot in range(2):
-            for j in range(2):
-                result = result + dot(act[3 * slot + j], weights[slot, side, 256 * j : 256 * j + 256, :])
-            result = result + dot(act[3 * slot + 2], weights[slot, 2, 256 * side : 256 * side + 256, :])
-        msg[:, 256 * side : 256 * side + 256] = result
-
-    live = live_ref[0] - hid * 512
+        cols = slice(256 * side, 256 * side + 256)
+        msg[:, cols] = msg[:, cols] + message_part(1, side)
+
     gain = gain_ref[...]
 
     def norm(i, carry):
         rows = pl.ds(pl.multiple_of(i * 64, 64), 64)
-        mask = (lax.broadcasted_iota(jnp.int32, (64, 512), 0) + i * 64) < live
-        upstream = jnp.where(mask, gedge[rows, :].astype(F32) + up[rows, :], 0.0)
-        up[rows, :] = upstream
+        upstream = up[rows, :]
         message = msg[rows, :]
         centre = message - jnp.mean(message, axis=1, keepdims=True)
         inverse = lax.rsqrt(jnp.mean(centre * centre, axis=1, keepdims=True) + EPS)
@@ -537,14 +560,11 @@
         tilt = jnp.mean(scaled * normed, axis=1, keepdims=True)
         grad = inverse * (scaled - shift - normed * tilt)
         low[rows, :] = grad.astype(BF16)
-
-        def fold(value):
-            return jnp.sum(value.reshape(8, 8, 512), axis=0)
-
-        return (carry[0] + fold(grad), carry[1] + fold(upstream * normed), carry[2] + fold(upstream))
+        return (carry[0] + fold(grad), carry[1] + fold(upstream * normed))
 
     zero = jnp.zeros((8, 512), F32)
-    vectors = lax.fori_loop(0, 8, norm, (zero, zero, zero))
+    vectors = lax.fori_loop(0, 8, norm, (zero, zero))
+    vectors = (*vectors, third_vector[...])
     sums[...] = jnp.zeros((16, 256), F32)
     for i in range(3):
         row = jnp.sum(vectors[i], axis=0, keepdims=True)
@@ -558,7 +578,10 @@
     halves = (hid, 1 - hid)
     for slot in range(2):
         for j in range(3):
-            part = tdot(act[3 * slot + j], low[...]).astype(BF16)
+            if slot == 0:
+                part = dot(act_turned[j], low[...]).astype(BF16)
+            else:
+                part = tdot(act[3 + j], low[...]).astype(BF16)
             if j < 2:
                 place_rows(grads, 0, 256 * j, part[:, 0:256], halves[slot])
                 place_rows(grads, 1, 256 * j, part[:, 256:512], halves[slot])
@@ -849,6 +872,8 @@
             pltpu.VMEM((2, 64, 512), BF16),
             pltpu.VMEM((256, 256), BF16),
             pltpu.VMEM((256, 256), BF16),
+            pltpu.VMEM((8, 512), F32),
+            pltpu.VMEM((3, 256, 512), BF16),
             dma(6),
             dma(6, 8),
             dma(6, 8),

time: 82.6 us -> 81.5 us (0.987)
  Pallas kernels: 80.9 us -> 79.9 us
    pallas_call x1, Pallas kernels: 75.1 us -> 74.1 us  [per_device(): pl.pallas_call(main_kernel, out_shape=(shape((12, 512, 256), BF16), shape...]
where the time goes in v5:
time: 81.5 us; the launch traced here: 81.3 us
  Pallas kernels  79.9 us (98%)
  between operations  1.45 us (2%)
    pallas_call x1, Pallas kernels, per_device(): pl.pallas_call(main_kernel, out_shape=(shape((12, 512, 256), BF16), shape...  74.1 us
    pallas_call x1, Pallas kernels, per_device(): pl.pallas_call(finish_kernel, out_shape=(shape((768, 512), F32), shape((1...  5.81 us

profile of v5, /device:TPU:1, one launch (start us, length us, event | category | flops | bytes accessed | tf_op | source)
XLA Modules:
  0.0 81.3 jit_solution(14293128944984730855)
XLA Ops:
  1.3 74.1 %message_grads.1 = (bf16[12,512,256]{2,1,0:T(8,128)(2,1)}, bf16[512,512]{1,0:T(8,128)(2,1)}, bf16[256,256]{1,0:T(8,128)(2,1)}, f32[16,256]{1,0:T(8,128)}) custom-call(bf16[256,512]{1,0:T(8,128)(2,1)} %node_hbm.1, bf16[1024,512]{1,0:T(8,128)(2,1)} %edge_hbm.1, s32[2,64]{1,0:T(2,128)} %bitcast.16, s32[8,128]{1,0:T(8,128)} %bitcast.9, s32[8,128]{1,0:T(8,128)} %bitcast.10, ...), custom_call_target="tpu_custom_call" | custom-call | tf_op jit(solution)/shard_map/message_grads/pallas_call | solution.py:811
  75.4 5.8 %widen_grads.1 = (f32[768,512]{1,0:T(8,128)}, f32[1536,768]{1,0:T(8,128)}, f32[6,128]{1,0:T(8,128)}, f32[3,512]{1,0:T(4,128)}, bf16[512,512]{1,0:T(8,128)(2,1)}, /*index=5*/bf16[256,256]{1,0:T(8,128)(2,1)}) custom-call(bf16[12,512,256]{2,1,0:T(8,128)(2,1)} %get-tuple-element.16.total, bf16[512,512]{1,0:T(8,128)(2,1)} %get-tuple-element.17.edge_in, ...), custom_call_target="tpu_custom_call" | custom-call | tf_op jit(solution)/shard_map/widen_grads/pallas_call | solution.py:915

commit v6 on v5

--- a/solution.py
+++ b/solution.py
@@ -115,14 +115,22 @@
             self.steps[chunk] = gather_steps(place, chunk)
         halved = AXES[chunk][0] == "y"
         if step == 2:
-            first, count = ((1 - place.yl) * 16, 16) if halved else (0, 32)
-            self.send(chunk, 2, first, count, 6, place.other_core())
+            if halved:
+                self.send(chunk, 2, (1 - place.yl) * 16, 16, 6, place.other_core())
+                return
+            if (chunk, 1) not in self.flying:
+                self.send(chunk, 2, 0, 32, 6, place.other_core())
+                return
+            mine = getattr(place, AXES[chunk][0])
+            for at, j in enumerate((2, 1, 3)):
+                self.flying[chunk, 1][at].wait_recv()
+                self.send(chunk, 2, lax.rem(mine + 4 - j, 4) * 8, 8, 6 + at, place.other_core())
             return
         first, count, targets = self.steps[chunk][step]
         for j, target in enumerate(targets):
             self.send(chunk, step, first, count, 3 * step + j, target)
-        if step == 1 and halved:
-            self.send(chunk, 2, first, count, 7, place.other_core())
+        if step == 1:
+            self.send(chunk, 2, first, count, 9, place.other_core())
 
     def send(self, chunk, step, first, count, index, target):
         block = 2 * chunk + self.place.core
@@ -133,6 +141,8 @@
         self.flying.setdefault((chunk, step), []).append(copy)
 
     def arrived(self, chunk, step):
+        if step == 1 and AXES[chunk][0] != "y":
+            return
         for copy in self.flying[chunk, step]:
             copy.wait_recv()
 
@@ -875,16 +885,16 @@
             pltpu.VMEM((8, 512), F32),
             pltpu.VMEM((3, 256, 512), BF16),
             dma(6),
-            dma(6, 8),
-            dma(6, 8),
+            dma(6, 10),
+            dma(6, 10),
             dma(7),
             dma(7),
             dma(2),
             dma(2),
             dma(6, 10),
             dma(6, 10),
-            dma(6, 8),
-            dma(6, 8),
+            dma(6, 10),
+            dma(6, 10),
             dma(4, 4),
             dma(4, 4),
             dma(3),

time: 81.5 us -> 81.7 us (level)
  no operation moved by 1% of the time
where the time goes in v6:
time: 81.7 us; the launch traced here: 81.5 us
  Pallas kernels  80 us (98%)
  between operations  1.45 us (2%)
    pallas_call x1, Pallas kernels, per_device(): pl.pallas_call(main_kernel, out_shape=(shape((12, 512, 256), BF16), shape...  74.2 us
    pallas_call x1, Pallas kernels, per_device(): pl.pallas_call(finish_kernel, out_shape=(shape((768, 512), F32), shape((1...  5.81 us

profile of v6, /device:TPU:1, one launch (start us, length us, event | category | flops | bytes accessed | tf_op | source)
XLA Modules:
  0.0 81.5 jit_solution(5262561200254202656)
XLA Ops:
  1.3 74.2 %message_grads.1 = (bf16[12,512,256]{2,1,0:T(8,128)(2,1)}, bf16[512,512]{1,0:T(8,128)(2,1)}, bf16[256,256]{1,0:T(8,128)(2,1)}, f32[16,256]{1,0:T(8,128)}) custom-call(bf16[256,512]{1,0:T(8,128)(2,1)} %node_hbm.1, bf16[1024,512]{1,0:T(8,128)(2,1)} %edge_hbm.1, s32[2,64]{1,0:T(2,128)} %bitcast.16, s32[8,128]{1,0:T(8,128)} %bitcast.9, s32[8,128]{1,0:T(8,128)} %bitcast.10, ...), custom_call_target="tpu_custom_call" | custom-call | tf_op jit(solution)/shard_map/message_grads/pallas_call | solution.py:821
  75.5 5.8 %widen_grads.1 = (f32[768,512]{1,0:T(8,128)}, f32[1536,768]{1,0:T(8,128)}, f32[6,128]{1,0:T(8,128)}, f32[3,512]{1,0:T(4,128)}, bf16[512,512]{1,0:T(8,128)(2,1)}, /*index=5*/bf16[256,256]{1,0:T(8,128)(2,1)}) custom-call(bf16[12,512,256]{2,1,0:T(8,128)(2,1)} %get-tuple-element.16.total, bf16[512,512]{1,0:T(8,128)(2,1)} %get-tuple-element.17.edge_in, ...), custom_call_target="tpu_custom_call" | custom-call | tf_op jit(solution)/shard_map/widen_grads/pallas_call | solution.py:925
